TPU v7x, 32 devices: a whole 2x2x4 slice. The times are simulated.
32 devices in a mesh: group: 4 (over y, x), member: 8 (over z, core).
Axes of the slice: x: 2, y: 2, z: 4, core: 2. Of those that a mesh axis runs over, the one named last changes fastest.
Arguments:
- old_ids: int32 [512], P(('group', 'member')), may hold values from -1 to 255, as said below
- field_old: float32 [512, 32, 1024], P(('group', 'member')), may hold values from -6 to 6
- source_old: float32 [512, 32, 1024], P(('group', 'member')), may hold values from -12 to 12
- kappa_old: float32 [512, 32, 1024], P(('group', 'member')), may hold values from 0.5 to 5
- refine: int32 [256], P(('group', 'member')), may hold values 0 or 1
- neighbors: int32 [256, 6], P(('group', 'member')), may hold values from -1 to 255, as said below
- coarse_inverse: float32 [4, 512, 512], P('group', 'member'), may hold values from -0.0546875 to 0.0546875
Outputs:
- solution: float32 [256, 32, 1024], P(('group', 'member'))
Inputs may be any that keep to these rules, and one draw needn't show every extreme that they name: `old_ids`: on each device the live slots come first and hold consecutive curve indices in increasing order, devices following one another along the curve; every block's new owner (index // 8) is the device that holds it or the next one; some device fills all 16 slots. Blocks form a grid in Morton order (bit i of a curve index is a bit of coordinate i mod 3); neighbors[g, k] is either -1 or the block adjacent to g across face k in that grid; relations are mutual: neighbors[g, k] = h means neighbors[h, k xor 1] = g.
All inputs are finite; a program needn't handle non-finite values. No bound on the sum of `refine` on one device may be relied on, other than what follows from the above.
Results may differ from a plain program's by a relative error of at most 0.000078.
Values sent between devices are 32-bit elements; how exact they have to be, the bound alone decides.
A program may use at most 128 MiB of HBM per device.

v0:
```python
import functools

import jax
import jax.numpy as jnp
from jax import lax
from jax.experimental import pallas as pl
from jax.experimental.pallas import tpu as pltpu
from jax.sharding import PartitionSpec as P

OMEGA = 0.8
AXES = ("group", "member")
NB, EDGE, FACE = 8, 32, 1024
HIGHEST = lax.Precision.HIGHEST
VMEM_LIMIT = 56 * 2**20
VM = pl.BlockSpec(memory_space=pltpu.VMEM)
ANY = pl.BlockSpec(memory_space=pl.ANY)
MESH = pl.DeviceIdType.MESH
SM = pl.BlockSpec(memory_space=pltpu.SMEM)
FACE_SHAPES = ((4, FACE), (EDGE, 128), (8, FACE))


def roll(value, steps):
    width = value.shape[-1]
    return pltpu.roll(value, steps % width, value.ndim - 1)


def depth_lanes(shape):
    return lax.broadcasted_iota(jnp.int32, shape, len(shape) - 1) % EDGE


def blocks_of(axis, side):
    return [b for b in range(NB) if (b >> axis) % 2 == side]


def pack_faces(load, outs):
    segment = lax.broadcasted_iota(jnp.int32, (EDGE, 128), 1) // EDGE
    depth = depth_lanes((8, FACE))
    everything = slice(0, FACE)
    for side in (0, 1):
        for j, b in enumerate(blocks_of(0, side)):
            row = (EDGE - 1) * side
            outs[0][side][j : j + 1, :] = load(b, slice(row, row + 1), everything)
        packed = jnp.zeros((EDGE, 128), jnp.float32)
        for j, b in enumerate(blocks_of(1, side)):
            low = (FACE - 128) * side
            piece = load(b, slice(0, EDGE), slice(low, low + 128))
            packed = jnp.where(segment == j, roll(piece, EDGE * (j - 3 * side)), packed)
        outs[1][side][...] = packed
        packed = jnp.zeros((8, FACE), jnp.float32)
        for j, b in enumerate(blocks_of(2, side)):
            for part in range(4):
                slot = 4 * j + part
                piece = load(b, slice(8 * part, 8 * part + 8), everything)
                packed = jnp.where(depth == slot, roll(piece, slot - 31 * side), packed)
        outs[2][side][...] = packed


def fill(values, ghosts, nbrs, pad, sheet, mirror):
    everything = slice(0, FACE)
    depth = depth_lanes((8, FACE))
    for b in range(NB):
        pad[b, 8:40, 128 : 128 + FACE] = values[b]
        for side in (0, 1):
            inside = [(b >> axis) % 2 != side for axis in range(3)]
            has = [nbrs[b, 2 * axis + side] >= 0 for axis in range(3)]
            j = [blocks_of(a, side).index(b) if not inside[a] else 0 for a in range(3)]
            row, far = (EDGE - 1) * side, (EDGE - 1) * (1 - side)
            if inside[0]:
                ghost = values[b ^ 1, far : far + 1, :]
            else:
                ghost = ghosts[0][side][j[0] : j[0] + 1, :]
            spare = values[b, row : row + 1, :] if mirror else jnp.zeros_like(ghost)
            place = 7 + 33 * side
            pad[b, place : place + 1, 128 : 128 + FACE] = jnp.where(has[0], ghost, spare)
            low, high = (FACE - 128) * side, (FACE - 128) * (1 - side)
            if inside[1]:
                ghost = values[b ^ 2, :, high : high + 128]
            else:
                ghost = roll(ghosts[1][side][...], EDGE * (3 * (1 - side) - j[1]))
            if mirror:
                spare = roll(values[b, :, low : low + 128], EDGE * (3 - 6 * side))
            else:
                spare = jnp.zeros_like(ghost)
            place = (128 + FACE) * side
            pad[b, 8:40, place : place + 128] = jnp.where(has[1], ghost, spare)
        for part in range(4):
            rows = slice(8 * part, 8 * part + 8)
            own = values[b, rows, :]
            near = []
            for side in (0, 1):
                if (b >> 2) % 2 != side:
                    ghost = roll(values[b ^ 4, rows, :], 31 * (2 * side - 1))
                else:
                    slot = 4 * blocks_of(2, side).index(b) + part
                    ghost = roll(ghosts[2][side][...], 31 * side - slot)
                spare = own if mirror else jnp.zeros_like(own)
                near.append(jnp.where(nbrs[b, 4 + side] >= 0, ghost, spare))
            sheet[b, rows, :] = jnp.where(depth < EDGE // 2, near[0], near[1])


def across(pad, sheet, b, part):
    depth = depth_lanes((8, FACE))
    top = 8 + 8 * part
    inner = slice(128, 128 + FACE)
    x_minus = pad[b, top - 1 : top + 7, inner]
    x_plus = pad[b, top + 1 : top + 9, inner]
    whole = pad[b, top : top + 8, :]
    edge = sheet[b, 8 * part : 8 * part + 8, :]
    y_minus = roll(whole, EDGE)[:, inner]
    y_plus = roll(whole, -EDGE)[:, inner]
    z_minus = jnp.where(depth == 0, edge, roll(whole, 1)[:, inner])
    z_plus = jnp.where(depth == EDGE - 1, edge, roll(whole, -1)[:, inner])
    return whole[:, inner], (x_minus, x_plus, y_minus, y_plus, z_minus, z_plus)


def face_partners(members, devices):
    here = lax.axis_index("group") * members + lax.axis_index("member")
    nbits = devices.bit_length() - 1
    bits = [here // 2**i % 2 for i in range(nbits)]
    result = []
    for axis in range(3):
        own = [i for i in range(nbits) if i % 3 == axis]
        extent = 2 ** len(own)
        coord = sum(bits[i] * 2**n for n, i in enumerate(own))
        base = here - sum(bits[i] * 2**i for i in own)
        pair = []
        for step in (-1, 1):
            moved = coord + step
            inside = jnp.logical_and(moved >= 0, moved < extent)
            clipped = jnp.clip(moved, 0, extent - 1)
            index = base + sum(clipped // 2**n % 2 * 2**i for n, i in enumerate(own))
            pair.append((inside, (index // members, index % members)))
        result.append(pair)
    return result


def main_kernel(
    members, devices, old_ids, nbrs, refine, inverse, u_old, f_old, k_old, out_ref, low_ref, high_ref, *scratch
):
    olds, stages, gots = scratch[0:3], scratch[3:6], scratch[6:9]
    u_ref, f_ref, k_ref, pad_u, sheet_u, pad_k, sheet_k, weights, sums, mine, all_sums = scratch[9:20]
    sent, ghost = [], []
    for phase in range(4):
        base = 20 + 6 * phase
        sent.append([[r.at[0], r.at[1]] for r in scratch[base : base + 3]])
        ghost.append([[r.at[0], r.at[1]] for r in scratch[base + 3 : base + 6]])
    in_sem, move_send, move_recv, face_send, face_recv, sum_send, sum_recv = scratch[44:51]

    member = lax.axis_index("member")
    here = lax.axis_index("group") * members + member
    partners = face_partners(members, devices)
    has_next, has_prev = here < devices - 1, here > 0
    after = jnp.minimum(here + 1, devices - 1)
    before = jnp.maximum(here - 1, 0)
    after = (after // members, after % members)
    before = (before // members, before % members)

    order = (0, 2, 1)
    loads = [
        pltpu.make_async_copy(ref, olds[i], in_sem.at[i])
        for i, ref in enumerate((u_old, f_old, k_old))
    ]
    for i in order:
        loads[i].start()

    barrier = pltpu.get_barrier_semaphore()
    expected = has_next.astype(jnp.int32) + (members - 1)
    for axis in range(3):
        for side in (0, 1):
            inside, peer = partners[axis][side]
            expected = expected + inside.astype(jnp.int32)

            @pl.when(inside)
            def _():
                pl.semaphore_signal(barrier, inc=1, device_id=peer, device_id_type=MESH)

    for step in range(1, members):
        pl.semaphore_signal(
            barrier,
            inc=1,
            device_id={"member": (member + step) % members},
            device_id_type=MESH,
        )

    @pl.when(has_prev)
    def _():
        pl.semaphore_signal(barrier, inc=1, device_id=before, device_id_type=MESH)

    kept = jnp.int32(0)
    for slot in range(2 * NB):
        index = old_ids[slot]
        own = jnp.logical_and(index >= here * NB, index < here * NB + NB)
        kept = kept + own.astype(jnp.int32)
    kept = jnp.minimum(kept, NB)
    count = NB - kept

    moves = [
        pltpu.make_async_remote_copy(
            src_ref=stages[i],
            dst_ref=gots[i],
            send_sem=move_send.at[i],
            recv_sem=move_recv.at[i],
            device_id=after,
            device_id_type=MESH,
        )
        for i in range(3)
    ]
    for i in order:
        loads[i].wait()

        def stage(p, carry, i=i):
            stages[i][p] = olds[i][kept + p]
            return carry

        lax.fori_loop(0, NB, stage, 0)
        if i == 0:
            pl.semaphore_wait(barrier, expected)

        @pl.when(has_next)
        def _():
            moves[i].start()

    def settle(i, out):
        @pl.when(has_prev)
        def _():
            moves[i].wait_recv()

        def body(p, carry):
            out[p] = jnp.where(p < count, gots[i][p], olds[i][jnp.maximum(p - count, 0)])
            return carry

        lax.fori_loop(0, NB, body, 0)

    def face_copy(phase, axis, side, peer):
        return pltpu.make_async_remote_copy(
            src_ref=sent[phase][axis][side],
            dst_ref=ghost[phase][axis][1 - side],
            send_sem=face_send.at[phase, 2 * axis + side],
            recv_sem=face_recv.at[phase, 2 * axis + 1 - side],
            device_id=peer,
            device_id_type=MESH,
        )

    def send_faces(phase, values):
        pack_faces(lambda b, rows, lanes: values[b, rows, lanes], sent[phase])
        for axis in range(3):
            for side in (0, 1):
                inside, peer = partners[axis][side]

                @pl.when(inside)
                def _():
                    face_copy(phase, axis, side, peer).start()

    def take_faces(phase):
        for axis in range(3):
            for side in (0, 1):
                inside, peer = partners[axis][side]

                @pl.when(inside)
                def _():
                    face_copy(phase, axis, side, peer).wait_send()
                    face_copy(phase, axis, 1 - side, peer).wait_recv()

    settle(0, u_ref)
    send_faces(0, u_ref)
    settle(2, k_ref)
    send_faces(3, k_ref)
    take_faces(0)
    fill(u_ref, ghost[0], nbrs, pad_u, sheet_u, False)
    take_faces(3)
    fill(k_ref, ghost[3], nbrs, pad_k, sheet_k, True)

    def weigh(b, carry):
        half_scale = 0.5 + 0.5 * refine[b].astype(jnp.float32)
        for part in range(4):
            rows = slice(8 * part, 8 * part + 8)
            k, around = across(pad_k, sheet_k, b, part)
            for face in range(6):
                weights[b, face, rows, :] = half_scale * (k + around[face])
        return carry

    lax.fori_loop(0, NB, weigh, 0)
    settle(1, f_ref)

    def terms(b, part, with_diagonal):
        rows = slice(8 * part, 8 * part + 8)
        u, around = across(pad_u, sheet_u, b, part)
        applied = jnp.zeros_like(u)
        diagonal = jnp.zeros_like(u)
        for face in range(6):
            weight = weights[b, face, rows, :]
            applied = applied + weight * (u - around[face])
            if with_diagonal:
                diagonal = diagonal + weight
        return u, f_ref[b, rows, :] - applied, diagonal

    def sweep(b, carry):
        for part in range(4):
            u, gap, diagonal = terms(b, part, True)
            u_ref[b, 8 * part : 8 * part + 8, :] = u + OMEGA * gap / diagonal
        return carry

    for phase in (1, 2):
        lax.fori_loop(0, NB, sweep, 0)
        send_faces(phase, u_ref)
        take_faces(phase)
        fill(u_ref, ghost[phase], nbrs, pad_u, sheet_u, False)

    def residual(b, carry):
        for half in (0, 1):
            gap = terms(b, 2 * half, False)[1] + terms(b, 2 * half + 1, False)[1]
            sums[2 * b + half] = gap
        return carry

    lax.fori_loop(0, NB, residual, 0)

    def cell_of(lane):
        return lane // (FACE // 2) * 2 + lane % EDGE // (EDGE // 2)

    choose = cell_of(lax.broadcasted_iota(jnp.int32, (FACE, 128), 0)) == lax.broadcasted_iota(
        jnp.int32, (FACE, 128), 1
    )
    rows = jnp.sum(sums[...], axis=1)
    mine[...] = jnp.dot(
        rows, choose.astype(jnp.float32), precision=HIGHEST, preferred_element_type=jnp.float32
    ) * (EDGE // 2) ** (-1.5)

    def sum_copy(step):
        return pltpu.make_async_remote_copy(
            src_ref=mine,
            dst_ref=all_sums.at[member],
            send_sem=sum_send.at[step],
            recv_sem=sum_recv.at[step],
            device_id={"member": (member + step) % members},
            device_id_type=MESH,
        )

    for step in range(1, members):
        sum_copy(step).start()
    all_sums[member] = mine[...]
    for step in range(1, members):
        sum_copy(step).wait_send()
        sum_copy(step).wait_recv()

    coarse = all_sums[...].reshape(members * 2 * NB, 128)
    cells = members * 8 * NB
    lane = lax.broadcasted_iota(jnp.int32, (128, cells), 1) % 4
    copies = (lane == lax.broadcasted_iota(jnp.int32, (128, cells), 0)).astype(jnp.float32)
    repeated = jnp.dot(coarse, copies, precision=HIGHEST, preferred_element_type=jnp.float32)
    owner = lax.broadcasted_iota(jnp.int32, repeated.shape, 1) // 4
    chosen = owner == lax.broadcasted_iota(jnp.int32, repeated.shape, 0)
    vector = jnp.sum(jnp.where(chosen, repeated, 0.0), axis=0, keepdims=True)
    column = jnp.sum(inverse[0] * vector, axis=1, keepdims=True)
    place = lax.broadcasted_iota(jnp.int32, (8 * NB, FACE), 0)
    cell = cell_of(lax.broadcasted_iota(jnp.int32, (8 * NB, FACE), 1))
    spread = jnp.where(place % 4 == cell, column, 0.0)
    rows_of = lax.broadcasted_iota(jnp.int32, (NB, 8 * NB), 1) // 4
    for half, rows_ref in ((0, low_ref), (1, high_ref)):
        wanted = 2 * lax.broadcasted_iota(jnp.int32, (NB, 8 * NB), 0) + half
        pick = (rows_of == wanted).astype(jnp.float32)
        rows_ref[...] = jnp.dot(
            pick, spread, precision=HIGHEST, preferred_element_type=jnp.float32
        )
    out_ref[...] = u_ref[...]

    @pl.when(has_next)
    def _():
        for i in order:
            moves[i].wait_send()


def local(old_ids, field_old, source_old, kappa_old, refine, neighbors, coarse_inverse):
    members = lax.axis_size("member")
    devices = lax.axis_size(AXES)
    whole = (NB, EDGE, FACE)
    shapes = [field_old.shape] * 3 + [whole] * 9
    padded = (NB, 48, FACE + 256)
    shapes += [padded, whole, padded, whole, (NB, 6, EDGE, FACE), (2 * NB, 8, FACE)]
    shapes += [(2 * NB, 128), (members, 2 * NB, 128)]
    shapes += [(2,) + s for _ in range(8) for s in FACE_SHAPES]
    dma = pltpu.SemaphoreType.DMA
    scratch = [pltpu.VMEM(s, jnp.float32) for s in shapes]
    scratch += [dma((3,)), dma((3,)), dma((3,)), dma((4, 6)), dma((4, 6))]
    scratch += [dma((members,)), dma((members,))]
    u, low, high = pl.pallas_call(
        functools.partial(main_kernel, members, devices),
        out_shape=[
            jax.ShapeDtypeStruct(whole, jnp.float32),
            jax.ShapeDtypeStruct((NB, FACE), jnp.float32),
            jax.ShapeDtypeStruct((NB, FACE), jnp.float32),
        ],
        in_specs=[SM, SM, SM, VM, ANY, ANY, ANY],
        out_specs=[VM, VM, VM],
        scratch_shapes=scratch,
        compiler_params=pltpu.CompilerParams(
            collective_id=1, has_side_effects=True, vmem_limit_bytes=VMEM_LIMIT
        ),
    )(old_ids, neighbors, refine, coarse_inverse, field_old, source_old, kappa_old)
    half = lax.broadcasted_iota(jnp.int32, (1, EDGE, 1), 1) < EDGE // 2
    return u + jnp.where(half, low[:, None, :], high[:, None, :])


def solution(mesh):
    in_specs = (
        P(AXES),
        P(AXES, None, None),
        P(AXES, None, None),
        P(AXES, None, None),
        P(AXES),
        P(AXES, None),
        P("group", "member", None),
    )
    return jax.shard_map(
        local, mesh=mesh, in_specs=in_specs, out_specs=P(AXES, None, None), check_vma=False
    )
```

profile of v0, /device:TPU:0, one launch (start us, length us, event | category | flops | bytes accessed | tf_op | source)
XLA Modules:
  0.0 72.3 jit_solution(2292947379046126262)
XLA Ops:
  0.0 69.8 %shard_map.73 = (f32[8,32,1024]{2,1,0:T(8,128)}, f32[8,1024]{1,0:T(8,128)}, f32[8,1024]{1,0:T(8,128)}) custom-call(s32[16]{0:T(128)} %old_ids.1, s32[8,6]{1,0:T(8,128)} %nbrs.1, s32[8]{0:T(128)} %refine.1, f32[1,64,512]{2,1,0:T(8,128)} %inverse.1, f32[16,32,1024]{2,1,0:T(8,128)} %u_old.1, f32[16,32,1024]{2,1,0:T(8,128)} %f_old.1, f32[16,32,1024]{2,1,0:T(8,128)} %k_old.1), custom_call_target="tpu_custom_call" | custom-call | tf_op jit(solution)/shard_map/pallas_call | solution.py:385
  69.9 2.5 %select_add_fusion = f32[8,32,1024]{2,1,0:T(8,128)} fusion(f32[8,32,1024]{2,1,0:T(8,128)} %get-tuple-element.8, f32[8,1024]{1,0:T(8,128)} %get-tuple-element.10, f32[8,1024]{1,0:T(8,128)} %get-tuple-element.9, pred[32]{0:T(512)(128)(4,1)S(1)} %iota_compare_fusion), kind=kLoop, calls=%fused_computation | loop fusion | flops 524288 | bytes 2162720 | tf_op jit(solution)/shard_map/add | solution.py:400
  (1 shorter events, 0.0 us)
where the time goes:
time: 72.5 us; the launch traced here: 72.3 us
  Pallas kernels  69.8 us (96%)
  other arithmetic  2.46 us (3%)
    pallas_call x1, Pallas kernels, local(): pl.pallas_call(functools.partial(main_kernel, members, devices), out_shap...  69.8 us
    add x1, other arithmetic, local(): return u + jnp.where(half, low[:, None, :], high[:, None, :])  2.46 us

commit v1 on v0

v1 whole, which is shorter than its diff:
```python
import functools

import jax
import jax.numpy as jnp
from jax import lax
from jax.experimental import pallas as pl
from jax.experimental.pallas import tpu as pltpu
from jax.sharding import PartitionSpec as P

OMEGA = 0.8
AXES = ("group", "member")
NB, EDGE, FACE, LANES = 8, 32, 1024, 128
TILES, PARTS, PITCH = 8, 4, 48
HIGHEST = lax.Precision.HIGHEST
VMEM_LIMIT = 60 * 2**20
VM = pl.BlockSpec(memory_space=pltpu.VMEM)
ANY = pl.BlockSpec(memory_space=pl.ANY)
SM = pl.BlockSpec(memory_space=pltpu.SMEM)
MESH = pl.DeviceIdType.MESH
FIELDS = (2, 1, 1)


def roll(value, steps):
    return pltpu.roll(value, steps % LANES, 1)


def spot(tile, part):
    return slice(PITCH * (tile + 1) + 8 + 8 * part, PITCH * (tile + 1) + 16 + 8 * part)


def flat(tile, part):
    return slice(EDGE * tile + 8 * part, EDGE * tile + 8 * part + 8)


def blocks_of(axis, side):
    return [b for b in range(NB) if (b >> axis) % 2 == side]


def octet_neighbors(octet, devices):
    nbits = devices.bit_length() - 1
    bits = [octet // 2**i % 2 for i in range(nbits)]
    result = []
    for axis in range(3):
        own = [i for i in range(nbits) if i % 3 == axis]
        extent = 2 ** len(own)
        coord = sum(bits[i] * 2**n for n, i in enumerate(own))
        base = octet - sum(bits[i] * 2**i for i in own)
        pair = []
        for step in (-1, 1):
            moved = coord + step
            inside = jnp.logical_and(moved >= 0, moved < extent)
            clipped = jnp.clip(moved, 0, extent - 1)
            index = base + sum(clipped // 2**n % 2 * 2**i for n, i in enumerate(own))
            pair.append((inside, index))
        result.append(pair)
    return result


def main_kernel(members, devices, old_ids, nbrs, refine, inverse, u_old, f_old, k_old, out_ref, *scratch):
    olds = scratch[0:3]
    u0, u1, k_ref, f_ref, omega, weight_sum, staged, moved, final_send, final_recv = scratch[3:13]
    send_out, own_in, recv_out, recv_in, ghosts = [scratch[13 + 3 * i : 16 + 3 * i] for i in range(5)]
    flags, acc, mine, all_sums, rows_e = scratch[28:33]
    in_sem, move_send, move_recv, out_send, out_recv, inner_send, inner_recv = scratch[33:40]
    flag_send, flag_recv, last_send, last_recv, sum_send, sum_recv = scratch[40:46]

    group, member = lax.axis_index("group"), lax.axis_index("member")
    here = group * members + member
    odd = here % 2 == 1
    even = here % 2 == 0
    has_q = here < devices - 1
    q_stays = jnp.logical_and(odd, has_q)
    p_split = jnp.logical_and(even, here > 0)
    around = [octet_neighbors(here, devices), octet_neighbors(here + 1, devices)]
    lane = lax.broadcasted_iota(jnp.int32, (8, LANES), 1)
    depth = lane % EDGE

    def where_is(index):
        return (index // members, index % members)

    loads = [
        pltpu.make_async_copy(ref, olds[i], in_sem.at[i]) for i, ref in enumerate((u_old, k_old, f_old))
    ]
    for load in loads:
        load.start()

    def both(*preds):
        result = preds[0]
        for pred in preds[1:]:
            result = jnp.logical_and(result, pred)
        return result

    outgoing, incoming = {}, {}
    for s in (0, 1):
        for axis in range(3):
            for side in (0, 1):
                inside, index = around[s][axis][side]
                exists = inside if s == 0 else both(inside, has_q)
                stays = inside if s == 0 else both(inside, q_stays)
                holder = both(index % 2 == 0, index > 0)
                for t in (0, 1):
                    target = index if t == 0 else jnp.maximum(index - 1, 0)
                    first = exists if t == 0 else both(exists, holder)
                    if s == 1 and t == 0 and axis == 0 and side == 0:
                        first = both(first, odd)
                    later = stays if t == 0 else both(stays, holder)
                    outgoing[s, axis, side, t] = (target, (first, later, later))
                receives = inside if s == 0 else both(inside, q_stays)
                for src in (0, 1):
                    source = index if src == 0 else jnp.maximum(index - 1, 0)
                    first = receives if src == 0 else both(receives, index > 0)
                    if s == 0 and src == 1 and axis == 0 and side == 1:
                        first = both(first, odd)
                    later = receives if src == 0 else both(receives, holder)
                    incoming[s, src, axis, side] = (source, (first, later, later))

    barrier = pltpu.get_barrier_semaphore()
    expected = jnp.int32(members - 1)
    for step in range(1, members):
        pl.semaphore_signal(
            barrier, inc=1, device_id={"member": (member + step) % members}, device_id_type=MESH
        )
    for target, preds in outgoing.values():
        expected = expected + both(preds[0], target // members != group).astype(jnp.int32)
    for source, preds in incoming.values():

        @pl.when(both(preds[0], source // members != group))
        def _():
            pl.semaphore_signal(barrier, inc=1, device_id=where_is(source), device_id_type=MESH)

    last = member == members - 1
    sends_last = both(last, has_q)
    gets_last = group > 0
    next_group = jnp.minimum(group + 1, devices // members - 1)
    prev_last = jnp.maximum(group * members - 1, 0)
    expected = expected + jnp.where(sends_last, members, 0)

    @pl.when(gets_last)
    def _():
        pl.semaphore_signal(barrier, inc=1, device_id=where_is(prev_last), device_id_type=MESH)

    first_in_group = both(member == 0, gets_last)
    expected = expected + first_in_group.astype(jnp.int32)

    @pl.when(sends_last)
    def _():
        pl.semaphore_signal(barrier, inc=1, device_id=(next_group, 0), device_id_type=MESH)

    kept, onward = jnp.int32(0), jnp.int32(0)
    for slot in range(2 * NB):
        index = old_ids[slot]
        kept = kept + both(index >= here * NB, index < here * NB + NB).astype(jnp.int32)
        onward = onward + (index >= here * NB + NB).astype(jnp.int32)
    kept = jnp.minimum(kept, NB)
    lacking = NB - kept

    for b in range(NB):
        for face in range(6):
            has = jnp.where(nbrs[b, face] >= 0, 1.0, 0.0).astype(jnp.float32)
            flags[b, face : face + 1, :] = jnp.full((1, LANES), has, jnp.float32)
        half_scale = 0.5 + 0.5 * refine[b].astype(jnp.float32)
        flags[b, 6:7, :] = jnp.full((1, LANES), half_scale, jnp.float32)
        flags[b, 7:8, :] = 1.0 / jnp.full((1, LANES), half_scale, jnp.float32)

    def settle(i, store):
        loads[i].wait()

        def own(p, carry):
            slot = jnp.maximum(p - lacking, 0)
            for tile in range(TILES):
                for part in range(PARTS):
                    value = olds[i][slot, 8 * part : 8 * part + 8, LANES * tile : LANES * (tile + 1)]
                    store(p, tile, part, jnp.where(p >= lacking, value, 0.0))
            return carry

        def following(p, carry):
            for tile in range(TILES):
                for part in range(PARTS):
                    value = olds[i][kept + p, 8 * part : 8 * part + 8, LANES * tile : LANES * (tile + 1)]
                    value = jnp.where(p < onward, value, 0.0)
                    store(NB + p, tile, part, value)
                    staged[i, p, flat(tile, part), :] = value
            return carry

        lax.fori_loop(0, NB, own, 0)
        lax.fori_loop(0, NB, following, 0)

    def pack(phase, s, field, volume, outer=True, inner=True):
        rows = EDGE * field

        def put(axis, side, bit, start, value):
            here_rows = pl.ds(rows + start, 8)
            if side == bit:
                send_out[phase][s, 2 * axis + side, here_rows, :] = value
            else:
                own_in[phase][s, bit, 3 * 0 + axis, here_rows, :] = value

        def wanted(side, bit):
            return outer if side == bit else inner

        for bit in (0, 1):
            for side in (0, 1):
                if not wanted(side, bit):
                    continue
                for j, b in enumerate(blocks_of(0, bit)):
                    line = volume[NB * s + b, pl.ds(PITCH + 8 + 31 * side, 8, stride=PITCH), :]
                    put(0, side, bit, 8 * j, line)
                for part in range(PARTS):
                    packed = jnp.zeros((8, LANES), jnp.float32)
                    for j, b in enumerate(blocks_of(1, bit)):
                        piece = volume[NB * s + b, spot(7 * side, part), :]
                        packed = jnp.where(lane // EDGE == j, roll(piece, EDGE * (j - 3 * side)), packed)
                    put(1, side, bit, 8 * part, packed)
            for quad in range(4):
                packed = [jnp.zeros((8, LANES), jnp.float32) for _ in (0, 1)]
                for half in (0, 1):
                    for j, b in enumerate(blocks_of(2, bit)):
                        for part in range(PARTS):
                            slot = 16 * half + 4 * j + part
                            piece = roll(volume[NB * s + b, spot(quad + 4 * half, part), :], slot)
                            for side in (0, 1):
                                if wanted(side, bit):
                                    packed[side] = jnp.where(
                                        depth == (slot + 31 * side) % EDGE, piece, packed[side]
                                    )
                for side in (0, 1):
                    if wanted(side, bit):
                        put(2, side, bit, 8 * quad, packed[side])

    def out_copy(phase, s, axis, side, t, target):
        return pltpu.make_async_remote_copy(
            src_ref=send_out[phase].at[s, 2 * axis + side],
            dst_ref=recv_out[phase].at[t, s, 2 * axis + 1 - side],
            send_sem=out_send.at[phase, s, 2 * axis + side, t],
            recv_sem=out_recv.at[phase, t, s, 2 * axis + 1 - side],
            device_id=where_is(target),
            device_id_type=MESH,
        )

    follower = jnp.minimum(here + 1, devices - 1)
    leader = jnp.maximum(here - 1, 0)

    def inner_copy(phase, s):
        return pltpu.make_async_remote_copy(
            src_ref=own_in[phase].at[s, 1 - s],
            dst_ref=recv_in[phase].at[1 - s],
            send_sem=inner_send.at[phase, s],
            recv_sem=inner_recv.at[phase, 1 - s],
            device_id=where_is(follower if s else leader),
            device_id_type=MESH,
        )

    flag_copy = pltpu.make_async_remote_copy(
        src_ref=flags.at[pl.ds(0, NB)],
        dst_ref=flags.at[pl.ds(NB, NB)],
        send_sem=flag_send,
        recv_sem=flag_recv,
        device_id=where_is(leader),
        device_id_type=MESH,
    )
    moves = [
        pltpu.make_async_remote_copy(
            src_ref=staged.at[i],
            dst_ref=moved.at[i],
            send_sem=move_send.at[i],
            recv_sem=move_recv.at[i],
            device_id=where_is(follower),
            device_id_type=MESH,
        )
        for i in range(3)
    ]

    def start_exchange(phase):
        for (s, axis, side, t), (target, preds) in outgoing.items():

            @pl.when(preds[phase])
            def _():
                out_copy(phase, s, axis, side, t, target).start()

        @pl.when(q_stays)
        def _():
            inner_copy(phase, 1).start()

        @pl.when(p_split)
        def _():
            inner_copy(phase, 0).start()

    def finish_exchange(phase):
        for (s, axis, side, t), (target, preds) in outgoing.items():

            @pl.when(preds[phase])
            def _():
                out_copy(phase, s, axis, side, t, target).wait_send()

        for (t, src, axis, side), (source, preds) in incoming.items():

            @pl.when(preds[phase])
            def _():
                out_copy(phase, src, axis, 1 - side, t, source).wait_recv()

        @pl.when(q_stays)
        def _():
            inner_copy(phase, 1).wait_send()
            inner_copy(phase, 0).wait_recv()

        @pl.when(p_split)
        def _():
            inner_copy(phase, 0).wait_send()
            inner_copy(phase, 1).wait_recv()

    def gather_ghosts(phase, t):
        split = (p_split, q_stays)[t]
        for axis in range(3):
            for side in (0, 1):
                face = 2 * axis + side
                total = 0.0
                for src in (0, 1):
                    pred = incoming[t, src, axis, side][1][phase]
                    if phase == 0 and (t, src, axis, side) == (0, 1, 0, 1):
                        own = jnp.where(even, send_out[0][1, 0], 0.0)
                        total = total + jnp.where(pred, recv_out[0][t, src, face], own)
                    else:
                        total = total + jnp.where(pred, recv_out[phase][t, src, face], 0.0)
                ghosts[phase][t, face] = total
                total = own_in[phase][t, side, axis]
                if side == t:
                    total = total + jnp.where(split, recv_in[phase][t, axis], 0.0)
                ghosts[phase][t, 6 + face] = total

    def fill(phase, q, field, volume, mirror):
        s, p = q // NB, q % NB
        rows = EDGE * field
        js = (p // 2, p % 2 + p // 4 * 2, p % 4)
        for side in (0, 1):
            kind = [jnp.where((p // 2**axis) % 2 == side, 0, 6) for axis in range(2)]
            ghost = ghosts[phase][s, kind[0] + side, pl.ds(pl.multiple_of(rows + 8 * js[0], 8), 8), :]
            has = flags[q, side : side + 1, :] > 0.5
            if mirror:
                spare = volume[q, pl.ds(PITCH + 8 + 31 * side, 8, stride=PITCH), :]
            else:
                spare = jnp.zeros_like(ghost)
            volume[q, pl.ds(PITCH + 7 + 33 * side, 8, stride=PITCH), :] = jnp.where(has, ghost, spare)
            has = flags[q, 2 + side : 3 + side, :] > 0.5
            for part in range(PARTS):
                ghost = ghosts[phase][s, kind[1] + 2 + side, rows + 8 * part : rows + 8 * part + 8, :]
                steps = EDGE * (3 - js[1]) if side == 0 else EDGE * ((4 - js[1]) % 4)
                ghost = pltpu.roll(ghost, steps, 1)
                if mirror:
                    spare = roll(volume[q, spot(7 * side, part), :], 96 - 64 * side)
                else:
                    spare = jnp.zeros_like(ghost)
                volume[q, spot(9 * side - 1, part), :] = jnp.where(has, ghost, spare)

    def stencil(phase, q, field, volume, mirror, part):
        s, p = q // NB, q % NB
        j = p % 4
        rows = EDGE * field
        bit = p // 4 % 2
        low_face = jnp.where(bit == 0, 0, 6) + 4
        high_face = jnp.where(bit == 1, 0, 6) + 5
        near = depth < EDGE // 2
        has = jnp.where(near, flags[q, 4:5, :], flags[q, 5:6, :]) > 0.5
        tiles = [volume[q, spot(t, part), :] for t in range(-1, TILES + 1)]
        down = [roll(t, EDGE) for t in tiles[:-1]]
        up = [None] + [roll(t, -EDGE) for t in tiles[1:]]
        for tile in range(TILES):
            value = tiles[tile + 1]
            top = PITCH * (tile + 1) + 8 + 8 * part
            x_minus = volume[q, top - 1 : top + 7, :]
            x_plus = volume[q, top + 1 : top + 9, :]
            y_minus = jnp.where(lane >= EDGE, down[tile + 1], down[tile])
            y_plus = jnp.where(lane < 3 * EDGE, up[tile + 1], up[tile + 2])
            base = 16 * (tile // 4) + part
            sheet = slice(rows + 8 * (tile % 4), rows + 8 * (tile % 4) + 8)
            low = pltpu.roll(ghosts[phase][s, low_face, sheet, :], 97 - base - 4 * j, 1)
            high = pltpu.roll(ghosts[phase][s, high_face, sheet, :], 31 - base - 4 * j, 1)
            edge = jnp.where(has, jnp.where(near, low, high), value if mirror else 0.0)
            z_minus = jnp.where(depth == 0, edge, roll(value, 1))
            z_plus = jnp.where(depth == EDGE - 1, edge, roll(value, -1))
            yield tile, value, (x_minus, x_plus, y_minus, y_plus, z_minus, z_plus)

    def valid(q):
        low = jnp.where(even, lacking, 0)
        return both(q >= low, q < NB + onward)

    def first_sweep(q, carry):
        fill(0, q, 0, u0, False)
        fill(0, q, 1, k_ref, True)
        holds = valid(q)
        for part in range(PARTS):
            pairs = zip(stencil(0, q, 0, u0, False, part), stencil(0, q, 1, k_ref, True, part))
            for (tile, u, u_beside), (_, k, k_beside) in pairs:
                weights = [k + beside for beside in k_beside]
                total = sum(weights[1:], weights[0])
                scale = jnp.where(holds, OMEGA / total, 0.0)
                place = flat(tile, part)
                weight_sum[q, place, :] = total * flags[q, 6:7, :] * (1.0 / OMEGA)
                gain = f_ref[q, place, :] * scale * flags[q, 7:8, :]
                f_ref[q, place, :] = gain
                new = (1.0 - OMEGA) * u + gain
                for face in range(6):
                    weight = weights[face] * scale
                    omega[q, face, place, :] = weight
                    new = new + weight * u_beside[face]
                u1[q, spot(tile, part), :] = new
        return carry

    def second_sweep(q, send):
        fill(1, q, 0, u1, False)
        for part in range(PARTS):
            for tile, u, beside in stencil(1, q, 0, u1, False, part):
                place = flat(tile, part)
                new = (1.0 - OMEGA) * u + f_ref[q, place, :]
                for face in range(6):
                    new = new + omega[q, face, place, :] * beside[face]
                u0[q, spot(tile, part), :] = new
                if send:
                    final_send[q - NB, place, :] = new

    def residual(q, carry):
        fill(2, q, 0, u0, False)
        totals = [jnp.zeros((8, LANES), jnp.float32) for _ in range(4)]
        for part in range(PARTS):
            for tile, u, beside in stencil(2, q, 0, u0, False, part):
                place = flat(tile, part)
                change = f_ref[q, place, :] - OMEGA * u
                for face in range(6):
                    change = change + omega[q, face, place, :] * beside[face]
                cell = part // 2 * 2 + tile // 4
                totals[cell] = totals[cell] + change * weight_sum[q, place, :]
        holds = valid(q)
        for cell in range(4):
            acc[4 * q + cell] = jnp.where(holds, totals[cell], 0.0)
        return carry

    sets = jnp.where(odd, 2, 1)
    blocks = NB * sets

    def pack_all(phase, field, volume):
        def body(s, carry):
            pack(phase, s, field, volume)
            return carry

        lax.fori_loop(0, 2 if phase == 0 else sets, body, 0)

    def gather_all(phase):
        gather_ghosts(phase, 0)

        @pl.when(odd)
        def _():
            gather_ghosts(phase, 1)

    def to_volume(volume):
        def store(q, tile, part, value):
            volume[q, spot(tile, part), :] = value

        return store

    def to_source(q, tile, part, value):
        f_ref[q, flat(tile, part), :] = value

    settle(0, to_volume(u0))
    pack_all(0, 0, u0)
    settle(1, to_volume(k_ref))
    pack_all(0, 1, k_ref)
    pl.semaphore_wait(barrier, expected)
    start_exchange(0)

    @pl.when(p_split)
    def _():
        flag_copy.start()

    @pl.when(even)
    def _():
        moves[0].start()
        moves[1].start()

    settle(2, to_source)

    @pl.when(even)
    def _():
        moves[2].start()

    @pl.when(odd)
    def _():
        for i in range(3):
            moves[i].wait_recv()

        def merge(p, carry):
            for tile in range(TILES):
                for part in range(PARTS):
                    for i, volume in enumerate((u0, k_ref)):
                        volume[p, spot(tile, part), :] += moved[i, p, flat(tile, part), :]
                    f_ref[p, flat(tile, part), :] += moved[2, p, flat(tile, part), :]
            return carry

        lax.fori_loop(0, NB, merge, 0)
        pack(0, 0, 0, u0, outer=False)
        pack(0, 0, 1, k_ref, outer=False)

    finish_exchange(0)

    @pl.when(p_split)
    def _():
        flag_copy.wait_send()

    @pl.when(q_stays)
    def _():
        flag_copy.wait_recv()

    gather_all(0)
    lax.fori_loop(0, blocks, first_sweep, 0)

    pack_all(1, 0, u1)
    start_exchange(1)
    finish_exchange(1)
    gather_all(1)

    def final_copy(p):
        return pltpu.make_async_remote_copy(
            src_ref=final_send.at[p],
            dst_ref=final_recv.at[p],
            send_sem=last_send.at[p],
            recv_sem=last_recv.at[p],
            device_id=where_is(follower),
            device_id_type=MESH,
        )

    @pl.when(odd)
    def _():
        def body(q, carry):
            second_sweep(q, True)

            @pl.when(has_q)
            def _():
                final_copy(q - NB).start()

            return carry

        lax.fori_loop(NB, 2 * NB, body, 0)

    def body(q, carry):
        second_sweep(q, False)
        return carry

    lax.fori_loop(0, NB, body, 0)

    pack_all(2, 0, u0)
    start_exchange(2)
    finish_exchange(2)
    gather_all(2)
    lax.fori_loop(0, blocks, residual, 0)

    sums = jnp.sum(acc[...], axis=1)
    halves = lax.broadcasted_iota(jnp.int32, (LANES, LANES), 0) % EDGE // (EDGE // 2)
    choose = halves == lax.broadcasted_iota(jnp.int32, (LANES, LANES), 1) % 2
    cells = jnp.dot(
        sums, choose.astype(jnp.float32), precision=HIGHEST, preferred_element_type=jnp.float32
    )
    row = lax.broadcasted_iota(jnp.int32, (8 * NB, LANES), 0)
    column = lax.broadcasted_iota(jnp.int32, (8 * NB, LANES), 1) // 2
    odd_int = odd.astype(jnp.int32)
    picked = jnp.logical_and((row + 32 * odd_int) % 64 == column, row < 32 + 32 * odd_int)
    total = jnp.sum(jnp.where(picked, cells, 0.0), axis=0, keepdims=True)
    mine[...] = jnp.broadcast_to(total * (EDGE // 2) ** (-1.5), (8, LANES))

    def sum_copy(step):
        return pltpu.make_async_remote_copy(
            src_ref=mine,
            dst_ref=all_sums.at[member],
            send_sem=sum_send.at[step],
            recv_sem=sum_recv.at[step],
            device_id={"member": (member + step) % members},
            device_id_type=MESH,
        )

    def on_copy(step):
        return pltpu.make_async_remote_copy(
            src_ref=mine,
            dst_ref=all_sums.at[members],
            send_sem=sum_send.at[members + step],
            recv_sem=sum_recv.at[0],
            device_id=(next_group, step),
            device_id_type=MESH,
        )

    for step in range(1, members):
        sum_copy(step).start()

    @pl.when(sends_last)
    def _():
        for step in range(members):
            on_copy(step).start()

    all_sums[member] = mine[...]
    for step in range(1, members):
        sum_copy(step).wait_send()
        sum_copy(step).wait_recv()

    @pl.when(sends_last)
    def _():
        for step in range(members):
            on_copy(step).wait_send()

    @pl.when(gets_last)
    def _():
        on_copy(0).wait_recv()

    correction = jnp.zeros((8 * NB, LANES), jnp.float32)
    lane_row = lax.broadcasted_iota(jnp.int32, (1, LANES), 1)
    for pair in range(members // 2):
        if pair == 0:
            before = jnp.where(gets_last, all_sums[members, 0:1, :], 0.0)
        else:
            before = all_sums[2 * pair - 1, 0:1, :]
        even_cells = all_sums[2 * pair, 0:1, :] + before
        vector = jnp.where(lane_row < 64, even_cells, all_sums[2 * pair + 1, 0:1, :])
        correction = correction + inverse[0, :, LANES * pair : LANES * (pair + 1)] * vector
    rows_e[...] = jnp.broadcast_to(jnp.sum(correction, axis=1, keepdims=True), (8 * NB, LANES))

    @pl.when(p_split)
    def _():
        for p in range(NB):
            final_copy(p).wait_recv()

    def finish(p, carry):
        for cell in range(4):
            first = pl.multiple_of(8 * p, 8) + 2 * cell
            lift = jnp.where(depth < EDGE // 2, rows_e[pl.ds(first, 1), :], rows_e[pl.ds(first + 1, 1), :])
            for part in (2 * (cell // 2), 2 * (cell // 2) + 1):
                for tile in range(4 * (cell % 2), 4 * (cell % 2) + 4):
                    arrived = jnp.where(p_split, final_recv[p, flat(tile, part), :], 0.0)
                    value = u0[p, spot(tile, part), :] + arrived + lift
                    out_ref[p, 8 * part : 8 * part + 8, LANES * tile : LANES * (tile + 1)] = value
        return carry

    lax.fori_loop(0, NB, finish, 0)

    @pl.when(even)
    def _():
        for i in range(3):
            moves[i].wait_send()

    @pl.when(q_stays)
    def _():
        for p in range(NB):
            final_copy(p).wait_send()


def local(old_ids, field_old, source_old, kappa_old, refine, neighbors, coarse_inverse):
    members = lax.axis_size("member")
    devices = lax.axis_size(AXES)
    flat_shape = (NB, TILES * EDGE, LANES)
    both_shape = (2 * NB, TILES * EDGE, LANES)
    padded = (2 * NB, 10 * PITCH, LANES)
    shapes = [field_old.shape] * 3 + [padded] * 3 + [both_shape]
    shapes += [(2 * NB, 6, TILES * EDGE, LANES), both_shape, (3,) + flat_shape, (3,) + flat_shape]
    shapes += [flat_shape, flat_shape]
    shapes += [(2, 6, EDGE * n, LANES) for n in FIELDS]
    shapes += [(2, 2, 3, EDGE * n, LANES) for n in FIELDS]
    shapes += [(2, 2, 6, EDGE * n, LANES) for n in FIELDS]
    shapes += [(2, 3, EDGE * n, LANES) for n in FIELDS]
    shapes += [(2, 12, EDGE * n, LANES) for n in FIELDS]
    shapes += [(2 * NB, 8, LANES), (8 * NB, 8, LANES), (8, LANES), (members + 1, 8, LANES)]
    shapes += [(8 * NB, LANES)]
    dma = pltpu.SemaphoreType.DMA
    scratch = [pltpu.VMEM(s, jnp.float32) for s in shapes]
    scratch += [dma((3,)), dma((3,)), dma((3,)), dma((3, 2, 6, 2)), dma((3, 2, 2, 6))]
    scratch += [dma((3, 2)), dma((3, 2)), dma, dma, dma((NB,)), dma((NB,))]
    scratch += [dma((2 * members,)), dma((members,))]
    return pl.pallas_call(
        functools.partial(main_kernel, members, devices),
        out_shape=jax.ShapeDtypeStruct((NB, EDGE, FACE), jnp.float32),
        in_specs=[SM, SM, SM, VM, ANY, ANY, ANY],
        out_specs=VM,
        scratch_shapes=scratch,
        compiler_params=pltpu.CompilerParams(
            collective_id=1, has_side_effects=True, vmem_limit_bytes=VMEM_LIMIT
        ),
    )(old_ids, neighbors, refine, coarse_inverse, field_old, source_old, kappa_old)


def solution(mesh):
    in_specs = (
        P(AXES),
        P(AXES, None, None),
        P(AXES, None, None),
        P(AXES, None, None),
        P(AXES),
        P(AXES, None),
        P("group", "member", None),
    )
    return jax.shard_map(
        local, mesh=mesh, in_specs=in_specs, out_specs=P(AXES, None, None), check_vma=False
    )
```

time: 72.5 us -> 66.2 us (0.913)
  the two profiles are of different devices: /device:TPU:0 before, /device:TPU:4 now
where the time goes in v1:
time: 66.2 us; the launch traced here: 65.7 us
  Pallas kernels  63.4 us (96%)
  local copies, waits for them, and re-layouts  2.31 us (3%)
    pallas_call x1, Pallas kernels, local(): pl.pallas_call(functools.partial(main_kernel, members, devices), out_shap...  63.4 us
    unnamed x1, local copies, waits for them, and re-layouts  2.31 us

profile of v1, /device:TPU:4, one launch (start us, length us, event | category | flops | bytes accessed | tf_op | source)
XLA Modules:
  0.0 65.7 jit_solution(1716068563265131167)
XLA Ops:
  0.0 63.4 %shard_map.73 = f32[8,32,1024]{2,1,0:T(8,128)} custom-call(s32[16]{0:T(128)} %old_ids.1, s32[8,6]{1,0:T(8,128)} %nbrs.1, s32[8]{0:T(128)} %refine.1, f32[1,64,512]{2,1,0:T(8,128)} %inverse.1, f32[16,32,1024]{2,1,0:T(8,128)} %u_old.1, f32[16,32,1024]{2,1,0:T(8,128)} %f_old.1, f32[16,32,1024]{2,1,0:T(8,128)} %k_old.1), custom_call_target="tpu_custom_call" | custom-call | tf_op jit(solution)/shard_map/pallas_call | solution.py:671
  63.4 2.3 %copy.9 = f32[8,32,1024]{2,1,0:T(8,128)} copy(f32[8,32,1024]{2,1,0:T(8,128)} %shard_map.73) | data formatting | bytes 2097152

commit v2 on v1

--- a/solution.py
+++ b/solution.py
@@ -18,6 +18,7 @@
 SM = pl.BlockSpec(memory_space=pltpu.SMEM)
 MESH = pl.DeviceIdType.MESH
 FIELDS = (2, 1, 1)
+EARLY = 4
 
 
 def roll(value, steps):
@@ -531,7 +532,7 @@
         def body(q, carry):
             second_sweep(q, True)
 
-            @pl.when(has_q)
+            @pl.when(both(has_q, q < NB + EARLY))
             def _():
                 final_copy(q - NB).start()
 
@@ -547,6 +548,12 @@
 
     pack_all(2, 0, u0)
     start_exchange(2)
+
+    @pl.when(q_stays)
+    def _():
+        for p in range(EARLY, NB):
+            final_copy(p).start()
+
     finish_exchange(2)
     gather_all(2)
     lax.fori_loop(0, blocks, residual, 0)

time: 66.2 us -> 63.4 us (0.958)
  the two profiles are of different devices: /device:TPU:4 before, /device:TPU:11 now
where the time goes in v2:
time: 63.4 us; the launch traced here: 63.2 us
  Pallas kernels  60.9 us (96%)
  local copies, waits for them, and re-layouts  2.31 us (4%)
    pallas_call x1, Pallas kernels, local(): pl.pallas_call(functools.partial(main_kernel, members, devices), out_shap...  60.9 us
    unnamed x1, local copies, waits for them, and re-layouts  2.31 us

profile of v2, /device:TPU:11, one launch (start us, length us, event | category | flops | bytes accessed | tf_op | source)
XLA Modules:
  0.0 63.2 jit_solution(11822536771503786730)
XLA Ops:
  0.0 60.9 %shard_map.73 = f32[8,32,1024]{2,1,0:T(8,128)} custom-call(s32[16]{0:T(128)} %old_ids.1, s32[8,6]{1,0:T(8,128)} %nbrs.1, s32[8]{0:T(128)} %refine.1, f32[1,64,512]{2,1,0:T(8,128)} %inverse.1, f32[16,32,1024]{2,1,0:T(8,128)} %u_old.1, f32[16,32,1024]{2,1,0:T(8,128)} %f_old.1, f32[16,32,1024]{2,1,0:T(8,128)} %k_old.1), custom_call_target="tpu_custom_call" | custom-call | tf_op jit(solution)/shard_map/pallas_call | solution.py:678
  60.9 2.3 %copy.9 = f32[8,32,1024]{2,1,0:T(8,128)} copy(f32[8,32,1024]{2,1,0:T(8,128)} %shard_map.73) | data formatting | bytes 2097152

commit v3 on v2

--- a/solution.py
+++ b/solution.py
@@ -17,8 +17,9 @@
 ANY = pl.BlockSpec(memory_space=pl.ANY)
 SM = pl.BlockSpec(memory_space=pltpu.SMEM)
 MESH = pl.DeviceIdType.MESH
-FIELDS = (2, 1, 1)
-EARLY = 4
+FIELDS = (2, 1)
+EARLY, MIDDLE = 3, 5
+OWN, ALONG_X, ALONG_Y, ALONG_Z, SOURCE = range(5)
 
 
 def roll(value, steps):
@@ -60,10 +61,10 @@
 def main_kernel(members, devices, old_ids, nbrs, refine, inverse, u_old, f_old, k_old, out_ref, *scratch):
     olds = scratch[0:3]
     u0, u1, k_ref, f_ref, omega, weight_sum, staged, moved, final_send, final_recv = scratch[3:13]
-    send_out, own_in, recv_out, recv_in, ghosts = [scratch[13 + 3 * i : 16 + 3 * i] for i in range(5)]
-    flags, acc, mine, all_sums, rows_e = scratch[28:33]
-    in_sem, move_send, move_recv, out_send, out_recv, inner_send, inner_recv = scratch[33:40]
-    flag_send, flag_recv, last_send, last_recv, sum_send, sum_recv = scratch[40:46]
+    send_out, own_in, recv_out, recv_in, ghosts = [scratch[13 + 2 * i : 15 + 2 * i] for i in range(5)]
+    flags, acc, mine, all_sums, rows_e, edge_sums, got_sums, split_sums = scratch[23:31]
+    in_sem, move_send, move_recv, out_send, out_recv, inner_send, inner_recv = scratch[31:38]
+    flag_send, flag_recv, last_send, last_recv, sum_send, sum_recv = scratch[38:44]
 
     group, member = lax.axis_index("group"), lax.axis_index("member")
     here = group * members + member
@@ -115,6 +116,8 @@
                     later = receives if src == 0 else both(receives, holder)
                     incoming[s, src, axis, side] = (source, (first, later, later))
 
+    for b in range(NB):
+        flags[NB + b] = jnp.ones((8, LANES), jnp.float32)
     barrier = pltpu.get_barrier_semaphore()
     expected = jnp.int32(members - 1)
     for step in range(1, members):
@@ -229,11 +232,16 @@
                         put(2, side, bit, 8 * quad, packed[side])
 
     def out_copy(phase, s, axis, side, t, target):
+        face = 2 * axis + 1 - side
+        if phase == 2:
+            source, place = edge_sums.at[s], got_sums.at[t, s, face]
+        else:
+            source, place = send_out[phase].at[s, 2 * axis + side], recv_out[phase].at[t, s, face]
         return pltpu.make_async_remote_copy(
-            src_ref=send_out[phase].at[s, 2 * axis + side],
-            dst_ref=recv_out[phase].at[t, s, 2 * axis + 1 - side],
+            src_ref=source,
+            dst_ref=place,
             send_sem=out_send.at[phase, s, 2 * axis + side, t],
-            recv_sem=out_recv.at[phase, t, s, 2 * axis + 1 - side],
+            recv_sem=out_recv.at[phase, t, s, face],
             device_id=where_is(target),
             device_id_type=MESH,
         )
@@ -242,9 +250,13 @@
     leader = jnp.maximum(here - 1, 0)
 
     def inner_copy(phase, s):
+        if phase == 2:
+            source, place = edge_sums.at[s], split_sums.at[1 - s]
+        else:
+            source, place = own_in[phase].at[s, 1 - s], recv_in[phase].at[1 - s]
         return pltpu.make_async_remote_copy(
-            src_ref=own_in[phase].at[s, 1 - s],
-            dst_ref=recv_in[phase].at[1 - s],
+            src_ref=source,
+            dst_ref=place,
             send_sem=inner_send.at[phase, s],
             recv_sem=inner_recv.at[phase, 1 - s],
             device_id=where_is(follower if s else leader),
@@ -271,20 +283,17 @@
         for i in range(3)
     ]
 
-    def start_exchange(phase):
+    def start_exchange(phase, which):
         for (s, axis, side, t), (target, preds) in outgoing.items():
-
-            @pl.when(preds[phase])
-            def _():
-                out_copy(phase, s, axis, side, t, target).start()
-
-        @pl.when(q_stays)
+            if s == which:
+
+                @pl.when(preds[phase])
+                def _():
+                    out_copy(phase, s, axis, side, t, target).start()
+
+        @pl.when((p_split, q_stays)[which])
         def _():
-            inner_copy(phase, 1).start()
-
-        @pl.when(p_split)
-        def _():
-            inner_copy(phase, 0).start()
+            inner_copy(phase, which).start()
 
     def finish_exchange(phase):
         for (s, axis, side, t), (target, preds) in outgoing.items():
@@ -384,10 +393,14 @@
         low = jnp.where(even, lacking, 0)
         return both(q >= low, q < NB + onward)
 
+    def keep(kind, q, cell, value):
+        acc[pl.ds(pl.multiple_of(8 * (8 * NB * kind + 4 * q + cell), 8), 8), :] = value
+
     def first_sweep(q, carry):
         fill(0, q, 0, u0, False)
         fill(0, q, 1, k_ref, True)
         holds = valid(q)
+        totals = [jnp.zeros((8, LANES), jnp.float32) for _ in range(4)]
         for part in range(PARTS):
             pairs = zip(stencil(0, q, 0, u0, False, part), stencil(0, q, 1, k_ref, True, part))
             for (tile, u, u_beside), (_, k, k_beside) in pairs:
@@ -395,8 +408,11 @@
                 total = sum(weights[1:], weights[0])
                 scale = jnp.where(holds, OMEGA / total, 0.0)
                 place = flat(tile, part)
-                weight_sum[q, place, :] = total * flags[q, 6:7, :] * (1.0 / OMEGA)
-                gain = f_ref[q, place, :] * scale * flags[q, 7:8, :]
+                weight_sum[q, place, :] = total * (1.0 / OMEGA)
+                right = f_ref[q, place, :]
+                cell = part // 2 * 2 + tile // 4
+                totals[cell] = totals[cell] + right
+                gain = right * scale * flags[q, 7:8, :]
                 f_ref[q, place, :] = gain
                 new = (1.0 - OMEGA) * u + gain
                 for face in range(6):
@@ -404,45 +420,94 @@
                     omega[q, face, place, :] = weight
                     new = new + weight * u_beside[face]
                 u1[q, spot(tile, part), :] = new
+        for cell in range(4):
+            keep(SOURCE, q, cell, totals[cell])
         return carry
+
+    sublane = lax.broadcasted_iota(jnp.int32, (8, LANES), 0)
 
     def second_sweep(q, send):
         fill(1, q, 0, u1, False)
+        zero = jnp.zeros((8, LANES), jnp.float32)
+        along_z = [zero] * 4
+        along_y = {(layer, half): zero for layer in (0, 15, 16, 31) for half in (0, 1)}
         for part in range(PARTS):
             for tile, u, beside in stencil(1, q, 0, u1, False, part):
                 place = flat(tile, part)
                 new = (1.0 - OMEGA) * u + f_ref[q, place, :]
+                weights = [omega[q, face, place, :] for face in range(6)]
                 for face in range(6):
-                    new = new + omega[q, face, place, :] * beside[face]
+                    new = new + weights[face] * beside[face]
                 u0[q, spot(tile, part), :] = new
                 if send:
                     final_send[q - NB, place, :] = new
-
-    def residual(q, carry):
-        fill(2, q, 0, u0, False)
-        totals = [jnp.zeros((8, LANES), jnp.float32) for _ in range(4)]
-        for part in range(PARTS):
-            for tile, u, beside in stencil(2, q, 0, u0, False, part):
-                place = flat(tile, part)
-                change = f_ref[q, place, :] - OMEGA * u
-                for face in range(6):
-                    change = change + omega[q, face, place, :] * beside[face]
-                cell = part // 2 * 2 + tile // 4
-                totals[cell] = totals[cell] + change * weight_sum[q, place, :]
-        holds = valid(q)
-        for cell in range(4):
-            acc[4 * q + cell] = jnp.where(holds, totals[cell], 0.0)
-        return carry
-
-    sets = jnp.where(odd, 2, 1)
-    blocks = NB * sets
-
-    def pack_all(phase, field, volume):
+                scaled = new * weight_sum[q, place, :]
+                half, cell = part // 2, part // 2 * 2 + tile // 4
+                outward = jnp.where(depth % (EDGE // 2) == EDGE // 2 - 1, weights[5], weights[4])
+                along_z[cell] = along_z[cell] + outward * scaled
+                if tile in (0, 4):
+                    layer = 4 * tile
+                    along_y[layer, half] = along_y[layer, half] + weights[2] * scaled
+                if tile in (3, 7):
+                    layer = 4 * tile + 3
+                    along_y[layer, half] = along_y[layer, half] + weights[3] * scaled
+        for layer, half in along_y:
+            inside = lane < EDGE if layer in (0, 16) else lane >= 3 * EDGE
+            along_y[layer, half] = jnp.where(inside, along_y[layer, half], 0.0)
+        along_x = {}
+        for layer, face in ((0, 0), (15, 1), (16, 0), (31, 1)):
+            rows = pl.ds(layer, 8, stride=EDGE)
+            value = u0[q, pl.ds(PITCH + 8 + layer, 8, stride=PITCH), :]
+            along_x[layer] = omega[q, face, rows, :] * weight_sum[q, rows, :] * value
+        middle = along_x[15] - along_x[16]
+        own_x = (along_x[0] + middle, along_x[31] - middle)
+        for a in (0, 1):
+            middle = along_y[15, a] - along_y[16, a]
+            own_y = (along_y[0, a] + middle, along_y[31, a] - middle)
+            for b in (0, 1):
+                upper = sublane // 4 == b
+                keep(OWN, q, 2 * a + b, jnp.where(upper, own_x[a], 0.0) + own_y[b])
+                keep(ALONG_X, q, 2 * a + b, jnp.where(upper, along_x[31 * a], 0.0))
+                keep(ALONG_Y, q, 2 * a + b, along_y[31 * a, b])
+                keep(ALONG_Z, q, 2 * a + b, along_z[2 * a + b])
+
+    cell_lane = lax.broadcasted_iota(jnp.int32, (1, LANES), 1)
+    block_of = cell_lane // 8 % NB
+    corner = (cell_lane // 4 % 2, cell_lane // 2 % 2, cell_lane % 2)
+    wide = (LANES, LANES)
+    from_depth = lax.broadcasted_iota(jnp.int32, wide, 0) % EDGE
+    to_corner = lax.broadcasted_iota(jnp.int32, wide, 1) % 2
+    by_half = (from_depth // (EDGE // 2) == to_corner).astype(jnp.float32)
+
+    def one_at(level):
+        return (from_depth == level).astype(jnp.float32)
+
+    def take(value, choose):
+        return jnp.dot(value, choose, precision=HIGHEST, preferred_element_type=jnp.float32)
+
+    def sums_of(kind):
+        groups = []
+        for group in range(8):
+            start = 8 * (8 * NB * kind + 8 * group)
+            groups.append(sum(acc[pl.ds(start + i, 8, stride=8), :] for i in range(8)))
+        return jnp.concatenate(groups, axis=0)
+
+    def pick(value, s, block, place):
+        rows = lax.broadcasted_iota(jnp.int32, (4 * NB, LANES), 0)
+        part = value[4 * NB * s : 4 * NB * (s + 1), :]
+        return jnp.sum(jnp.where(rows == 4 * block + place, part, 0.0), axis=0, keepdims=True)
+
+    def other(axis):
+        bit = block_of // 2**axis % 2
+        return block_of + 2**axis * (1 - 2 * bit)
+
+
+    def pack_all(field, volume):
         def body(s, carry):
-            pack(phase, s, field, volume)
+            pack(0, s, field, volume)
             return carry
 
-        lax.fori_loop(0, 2 if phase == 0 else sets, body, 0)
+        lax.fori_loop(0, 2, body, 0)
 
     def gather_all(phase):
         gather_ghosts(phase, 0)
@@ -461,11 +526,12 @@
         f_ref[q, flat(tile, part), :] = value
 
     settle(0, to_volume(u0))
-    pack_all(0, 0, u0)
+    pack_all(0, u0)
     settle(1, to_volume(k_ref))
-    pack_all(0, 1, k_ref)
+    pack_all(1, k_ref)
     pl.semaphore_wait(barrier, expected)
-    start_exchange(0)
+    start_exchange(0, 1)
+    start_exchange(0, 0)
 
     @pl.when(p_split)
     def _():
@@ -510,10 +576,19 @@
         flag_copy.wait_recv()
 
     gather_all(0)
-    lax.fori_loop(0, blocks, first_sweep, 0)
-
-    pack_all(1, 0, u1)
-    start_exchange(1)
+
+    @pl.when(odd)
+    def _():
+        lax.fori_loop(NB, 2 * NB, first_sweep, 0)
+        pack(1, 1, 0, u1)
+        start_exchange(1, 1)
+
+    lax.fori_loop(0, NB, first_sweep, 0)
+    pack(1, 0, 0, u1)
+    start_exchange(1, 0)
+
+    cells = take(sums_of(SOURCE), by_half)
+    source_sums = [pick(cells, s, block_of, cell_lane // 2 % 4) for s in (0, 1)]
     finish_exchange(1)
     gather_all(1)
 
@@ -546,29 +621,60 @@
 
     lax.fori_loop(0, NB, body, 0)
 
-    pack_all(2, 0, u0)
-    start_exchange(2)
+    middle = take(jnp.concatenate([sums_of(kind) for kind in (OWN, ALONG_X, ALONG_Y)], axis=0), by_half)
+    crossing = one_at(15) - one_at(16)
+    low_cells, high_cells = one_at(0) + crossing, one_at(EDGE - 1) - crossing
+    z_sums = sums_of(ALONG_Z)
+    own_z = take(z_sums, jnp.where(to_corner == 0, low_cells, high_cells))
+    face_z = take(z_sums, jnp.where(to_corner == 0, one_at(EDGE - 1), one_at(0)))
+    size = 8 * NB
+    own_sums = []
+    for s in (0, 1):
+        own_sums.append(pick(middle[:size] + own_z, s, block_of, cell_lane // 2 % 4))
+        face_x = pick(middle[size : 2 * size], s, other(0), 2 * (1 - corner[0]) + corner[1])
+        face_y = pick(middle[2 * size :], s, other(1), 2 * (1 - corner[1]) + corner[0])
+        near_z = pick(face_z, s, other(2), cell_lane // 2 % 4)
+        edge_sums[s] = jnp.where(sublane == 0, face_x, jnp.where(sublane == 1, face_y, near_z))
+    start_exchange(2, 0)
+
+    @pl.when(odd)
+    def _():
+        start_exchange(2, 1)
 
     @pl.when(q_stays)
     def _():
-        for p in range(EARLY, NB):
+        for p in range(EARLY, MIDDLE):
             final_copy(p).start()
 
     finish_exchange(2)
-    gather_all(2)
-    lax.fori_loop(0, blocks, residual, 0)
-
-    sums = jnp.sum(acc[...], axis=1)
-    halves = lax.broadcasted_iota(jnp.int32, (LANES, LANES), 0) % EDGE // (EDGE // 2)
-    choose = halves == lax.broadcasted_iota(jnp.int32, (LANES, LANES), 1) % 2
-    cells = jnp.dot(
-        sums, choose.astype(jnp.float32), precision=HIGHEST, preferred_element_type=jnp.float32
-    )
-    row = lax.broadcasted_iota(jnp.int32, (8 * NB, LANES), 0)
-    column = lax.broadcasted_iota(jnp.int32, (8 * NB, LANES), 1) // 2
-    odd_int = odd.astype(jnp.int32)
-    picked = jnp.logical_and((row + 32 * odd_int) % 64 == column, row < 32 + 32 * odd_int)
-    total = jnp.sum(jnp.where(picked, cells, 0.0), axis=0, keepdims=True)
+    totals = []
+    for t in (0, 1):
+        combined = jnp.zeros((8, LANES), jnp.float32)
+        for p in range(NB):
+            combined = jnp.where(lane // 8 % NB == p, flags[NB * t + p], combined)
+        beyond = jnp.zeros((1, LANES), jnp.float32)
+        for axis in range(3):
+            row = slice(axis, axis + 1)
+            outer, linked = [], []
+            for side in (0, 1):
+                face = 2 * axis + side
+                total = 0.0
+                for src in (0, 1):
+                    pred = incoming[t, src, axis, side][1][2]
+                    total = total + jnp.where(pred, got_sums[t, src, face, row, :], 0.0)
+                outer.append(total)
+                linked.append(combined[face : face + 1, :])
+            split = jnp.where((p_split, q_stays)[t], split_sums[t, row, :], 0.0)
+            inner = edge_sums[t, row, :] + split
+            outer = jnp.where(corner[axis] == 0, outer[0], outer[1])
+            linked = jnp.where(corner[axis] == 0, linked[0], linked[1])
+            beside = jnp.where(block_of // 2**axis % 2 == corner[axis], outer, inner)
+            beyond = beyond + jnp.where(linked > 0.5, beside, 0.0)
+        held = block_of < onward if t else block_of >= jnp.where(even, lacking, 0)
+        change = combined[6:7, :] * (beyond - own_sums[t])
+        totals.append(jnp.where(held, source_sums[t] + change, 0.0))
+    low_half = jnp.where(odd, totals[1], totals[0])
+    total = jnp.where(cell_lane < 64, low_half, jnp.where(odd, totals[0], 0.0))
     mine[...] = jnp.broadcast_to(total * (EDGE // 2) ** (-1.5), (8, LANES))
 
     def sum_copy(step):
@@ -599,6 +705,11 @@
         for step in range(members):
             on_copy(step).start()
 
+    @pl.when(q_stays)
+    def _():
+        for p in range(MIDDLE, NB):
+            final_copy(p).start()
+
     all_sums[member] = mine[...]
     for step in range(1, members):
         sum_copy(step).wait_send()
@@ -614,14 +725,13 @@
         on_copy(0).wait_recv()
 
     correction = jnp.zeros((8 * NB, LANES), jnp.float32)
-    lane_row = lax.broadcasted_iota(jnp.int32, (1, LANES), 1)
     for pair in range(members // 2):
         if pair == 0:
             before = jnp.where(gets_last, all_sums[members, 0:1, :], 0.0)
         else:
             before = all_sums[2 * pair - 1, 0:1, :]
         even_cells = all_sums[2 * pair, 0:1, :] + before
-        vector = jnp.where(lane_row < 64, even_cells, all_sums[2 * pair + 1, 0:1, :])
+        vector = jnp.where(cell_lane < 64, even_cells, all_sums[2 * pair + 1, 0:1, :])
         correction = correction + inverse[0, :, LANES * pair : LANES * (pair + 1)] * vector
     rows_e[...] = jnp.broadcast_to(jnp.sum(correction, axis=1, keepdims=True), (8 * NB, LANES))
 
@@ -668,8 +778,8 @@
     shapes += [(2, 2, 6, EDGE * n, LANES) for n in FIELDS]
     shapes += [(2, 3, EDGE * n, LANES) for n in FIELDS]
     shapes += [(2, 12, EDGE * n, LANES) for n in FIELDS]
-    shapes += [(2 * NB, 8, LANES), (8 * NB, 8, LANES), (8, LANES), (members + 1, 8, LANES)]
-    shapes += [(8 * NB, LANES)]
+    shapes += [(2 * NB, 8, LANES), (5 * 64 * NB, LANES), (8, LANES), (members + 1, 8, LANES)]
+    shapes += [(8 * NB, LANES), (2, 8, LANES), (2, 2, 6, 8, LANES), (2, 8, LANES)]
     dma = pltpu.SemaphoreType.DMA
     scratch = [pltpu.VMEM(s, jnp.float32) for s in shapes]
     scratch += [dma((3,)), dma((3,)), dma((3,)), dma((3, 2, 6, 2)), dma((3, 2, 2, 6))]

time: 63.4 us -> 54.1 us (0.85)
  the two profiles are of different devices: /device:TPU:11 before, /device:TPU:4 now
where the time goes in v3:
time: 54.1 us; the launch traced here: 53.9 us
  Pallas kernels  51.6 us (95%)
  local copies, waits for them, and re-layouts  2.31 us (4%)
    pallas_call x1, Pallas kernels, local(): pl.pallas_call(functools.partial(main_kernel, members, devices), out_shap...  51.6 us
    unnamed x1, local copies, waits for them, and re-layouts  2.31 us

profile of v3, /device:TPU:4, one launch (start us, length us, event | category | flops | bytes accessed | tf_op | source)
XLA Modules:
  0.0 53.9 jit_solution(14013652679448232744)
XLA Ops:
  0.0 51.6 %shard_map.73 = f32[8,32,1024]{2,1,0:T(8,128)} custom-call(s32[16]{0:T(128)} %old_ids.1, s32[8,6]{1,0:T(8,128)} %nbrs.1, s32[8]{0:T(128)} %refine.1, f32[1,64,512]{2,1,0:T(8,128)} %inverse.1, f32[16,32,1024]{2,1,0:T(8,128)} %u_old.1, f32[16,32,1024]{2,1,0:T(8,128)} %f_old.1, f32[16,32,1024]{2,1,0:T(8,128)} %k_old.1), custom_call_target="tpu_custom_call" | custom-call | tf_op jit(solution)/shard_map/pallas_call | solution.py:788
  51.6 2.3 %copy.9 = f32[8,32,1024]{2,1,0:T(8,128)} copy(f32[8,32,1024]{2,1,0:T(8,128)} %shard_map.73) | data formatting | bytes 2097152

commit v4 on v3

--- a/solution.py
+++ b/solution.py
@@ -18,7 +18,7 @@
 SM = pl.BlockSpec(memory_space=pltpu.SMEM)
 MESH = pl.DeviceIdType.MESH
 FIELDS = (2, 1)
-EARLY, MIDDLE = 3, 5
+EARLY, MIDDLE = 4, 6
 OWN, ALONG_X, ALONG_Y, ALONG_Z, SOURCE = range(5)
 
 
@@ -63,8 +63,9 @@
     u0, u1, k_ref, f_ref, omega, weight_sum, staged, moved, final_send, final_recv = scratch[3:13]
     send_out, own_in, recv_out, recv_in, ghosts = [scratch[13 + 2 * i : 15 + 2 * i] for i in range(5)]
     flags, acc, mine, all_sums, rows_e, edge_sums, got_sums, split_sums = scratch[23:31]
-    in_sem, move_send, move_recv, out_send, out_recv, inner_send, inner_recv = scratch[31:38]
-    flag_send, flag_recv, last_send, last_recv, sum_send, sum_recv = scratch[38:44]
+    edges = scratch[31:33]
+    in_sem, move_send, move_recv, out_send, out_recv, inner_send, inner_recv = scratch[33:40]
+    flag_send, flag_recv, last_send, last_recv, sum_send, sum_recv = scratch[40:46]
 
     group, member = lax.axis_index("group"), lax.axis_index("member")
     here = group * members + member
@@ -83,8 +84,7 @@
     loads = [
         pltpu.make_async_copy(ref, olds[i], in_sem.at[i]) for i, ref in enumerate((u_old, k_old, f_old))
     ]
-    for load in loads:
-        load.start()
+    loads[0].start()
 
     def both(*preds):
         result = preds[0]
@@ -168,6 +168,8 @@
 
     def settle(i, store):
         loads[i].wait()
+        if i < 2:
+            loads[i + 1].start()
 
         def own(p, carry):
             slot = jnp.maximum(p - lacking, 0)
@@ -220,7 +222,7 @@
                 for half in (0, 1):
                     for j, b in enumerate(blocks_of(2, bit)):
                         for part in range(PARTS):
-                            slot = 16 * half + 4 * j + part
+                            slot = 8 * j + 2 * part + half
                             piece = roll(volume[NB * s + b, spot(quad + 4 * half, part), :], slot)
                             for side in (0, 1):
                                 if wanted(side, bit):
@@ -336,6 +338,15 @@
                 if side == t:
                     total = total + jnp.where(split, recv_in[phase][t, axis], 0.0)
                 ghosts[phase][t, 6 + face] = total
+        for bit in (0, 1):
+            low, high = (4 if bit == 0 else 10), (5 if bit == 1 else 11)
+            for chunk in range(4 * FIELDS[phase]):
+                rows = slice(8 * chunk, 8 * chunk + 8)
+                first = ghosts[phase][t, low, rows, :]
+                second = roll(ghosts[phase][t, high, rows, :], 62)
+                for half in (0, 1):
+                    both_ends = jnp.where(depth % 2 != half, first, second)
+                    edges[phase][t, 2 * bit + half, rows, :] = both_ends
 
     def fill(phase, q, field, volume, mirror):
         s, p = q // NB, q % NB
@@ -361,15 +372,15 @@
                     spare = jnp.zeros_like(ghost)
                 volume[q, spot(9 * side - 1, part), :] = jnp.where(has, ghost, spare)
 
-    def stencil(phase, q, field, volume, mirror, part):
+    def z_edge(phase, q, field, tile, part, spare):
         s, p = q // NB, q % NB
-        j = p % 4
-        rows = EDGE * field
-        bit = p // 4 % 2
-        low_face = jnp.where(bit == 0, 0, 6) + 4
-        high_face = jnp.where(bit == 1, 0, 6) + 5
-        near = depth < EDGE // 2
-        has = jnp.where(near, flags[q, 4:5, :], flags[q, 5:6, :]) > 0.5
+        start = EDGE * field + 8 * (tile % 4)
+        sheet = edges[phase][s, 2 * (p // 4) + tile // 4, start : start + 8, :]
+        ghost = pltpu.roll(sheet, 97 - 2 * part - tile // 4 - 8 * (p % 4), 1)
+        has = jnp.where(depth < EDGE // 2, flags[q, 4:5, :], flags[q, 5:6, :]) > 0.5
+        return jnp.where(has, ghost, spare)
+
+    def stencil(phase, q, volume, part):
         tiles = [volume[q, spot(t, part), :] for t in range(-1, TILES + 1)]
         down = [roll(t, EDGE) for t in tiles[:-1]]
         up = [None] + [roll(t, -EDGE) for t in tiles[1:]]
@@ -380,14 +391,41 @@
             x_plus = volume[q, top + 1 : top + 9, :]
             y_minus = jnp.where(lane >= EDGE, down[tile + 1], down[tile])
             y_plus = jnp.where(lane < 3 * EDGE, up[tile + 1], up[tile + 2])
-            base = 16 * (tile // 4) + part
-            sheet = slice(rows + 8 * (tile % 4), rows + 8 * (tile % 4) + 8)
-            low = pltpu.roll(ghosts[phase][s, low_face, sheet, :], 97 - base - 4 * j, 1)
-            high = pltpu.roll(ghosts[phase][s, high_face, sheet, :], 31 - base - 4 * j, 1)
-            edge = jnp.where(has, jnp.where(near, low, high), value if mirror else 0.0)
+            edge = z_edge(phase, q, 0, tile, part, 0.0)
             z_minus = jnp.where(depth == 0, edge, roll(value, 1))
             z_plus = jnp.where(depth == EDGE - 1, edge, roll(value, -1))
             yield tile, value, (x_minus, x_plus, y_minus, y_plus, z_minus, z_plus)
+
+    def weigh_inside(q, carry):
+        for part in range(PARTS):
+            tiles = [k_ref[q, spot(t, part), :] for t in range(TILES)]
+            down = [roll(t, EDGE) for t in tiles]
+            up = [roll(t, -EDGE) for t in tiles]
+            for tile in range(TILES):
+                place, k = flat(tile, part), tiles[tile]
+                before, after = down[max(tile - 1, 0)], up[min(tile + 1, TILES - 1)]
+                omega[q, 2, place, :] = k + jnp.where(lane >= EDGE, down[tile], before)
+                omega[q, 3, place, :] = k + jnp.where(lane < 3 * EDGE, up[tile], after)
+                omega[q, 4, place, :] = k + roll(k, 1)
+                omega[q, 5, place, :] = k + roll(k, -1)
+        return carry
+
+    def weigh(q, part):
+        before = roll(k_ref[q, spot(-1, part), :], EDGE)
+        after = roll(k_ref[q, spot(TILES, part), :], -EDGE)
+        for tile in range(TILES):
+            place, k = flat(tile, part), k_ref[q, spot(tile, part), :]
+            top = PITCH * (tile + 1) + 8 + 8 * part
+            around_k = [k_ref[q, top - 1 : top + 7, :], k_ref[q, top + 1 : top + 9, :]]
+            inside = [omega[q, face, place, :] for face in range(2, 6)]
+            if tile == 0:
+                inside[0] = jnp.where(lane >= EDGE, inside[0], k + before)
+            if tile == TILES - 1:
+                inside[1] = jnp.where(lane < 3 * EDGE, inside[1], k + after)
+            edge = k + z_edge(0, q, 1, tile, part, k)
+            inside[2] = jnp.where(depth == 0, edge, inside[2])
+            inside[3] = jnp.where(depth == EDGE - 1, edge, inside[3])
+            yield [k + beside for beside in around_k] + inside
 
     def valid(q):
         low = jnp.where(even, lacking, 0)
@@ -402,9 +440,7 @@
         holds = valid(q)
         totals = [jnp.zeros((8, LANES), jnp.float32) for _ in range(4)]
         for part in range(PARTS):
-            pairs = zip(stencil(0, q, 0, u0, False, part), stencil(0, q, 1, k_ref, True, part))
-            for (tile, u, u_beside), (_, k, k_beside) in pairs:
-                weights = [k + beside for beside in k_beside]
+            for (tile, u, u_beside), weights in zip(stencil(0, q, u0, part), weigh(q, part)):
                 total = sum(weights[1:], weights[0])
                 scale = jnp.where(holds, OMEGA / total, 0.0)
                 place = flat(tile, part)
@@ -432,7 +468,7 @@
         along_z = [zero] * 4
         along_y = {(layer, half): zero for layer in (0, 15, 16, 31) for half in (0, 1)}
         for part in range(PARTS):
-            for tile, u, beside in stencil(1, q, 0, u1, False, part):
+            for tile, u, beside in stencil(1, q, u1, part):
                 place = flat(tile, part)
                 new = (1.0 - OMEGA) * u + f_ref[q, place, :]
                 weights = [omega[q, face, place, :] for face in range(6)]
@@ -550,6 +586,7 @@
 
     @pl.when(odd)
     def _():
+        lax.fori_loop(NB, 2 * NB, weigh_inside, 0)
         for i in range(3):
             moves[i].wait_recv()
 
@@ -565,6 +602,7 @@
         pack(0, 0, 0, u0, outer=False)
         pack(0, 0, 1, k_ref, outer=False)
 
+    lax.fori_loop(0, NB, weigh_inside, 0)
     finish_exchange(0)
 
     @pl.when(p_split)
@@ -780,6 +818,7 @@
     shapes += [(2, 12, EDGE * n, LANES) for n in FIELDS]
     shapes += [(2 * NB, 8, LANES), (5 * 64 * NB, LANES), (8, LANES), (members + 1, 8, LANES)]
     shapes += [(8 * NB, LANES), (2, 8, LANES), (2, 2, 6, 8, LANES), (2, 8, LANES)]
+    shapes += [(2, 4, EDGE * n, LANES) for n in FIELDS]
     dma = pltpu.SemaphoreType.DMA
     scratch = [pltpu.VMEM(s, jnp.float32) for s in shapes]
     scratch += [dma((3,)), dma((3,)), dma((3,)), dma((3, 2, 6, 2)), dma((3, 2, 2, 6))]

time: 54.1 us -> 51.9 us (0.959)
  Pallas kernels: 51.6 us -> 49.2 us
    pallas_call x1, Pallas kernels: 51.6 us -> 49.2 us  [local(): pl.pallas_call(functools.partial(main_kernel, members, devices), out_shap...]
where the time goes in v4:
time: 51.9 us; the launch traced here: 51.5 us
  Pallas kernels  49.2 us (95%)
  local copies, waits for them, and re-layouts  2.31 us (4%)
    pallas_call x1, Pallas kernels, local(): pl.pallas_call(functools.partial(main_kernel, members, devices), out_shap...  49.2 us
    unnamed x1, local copies, waits for them, and re-layouts  2.31 us

profile of v4, /device:TPU:4, one launch (start us, length us, event | category | flops | bytes accessed | tf_op | source)
XLA Modules:
  0.0 51.5 jit_solution(14516835229885226828)
XLA Ops:
  0.0 49.2 %shard_map.73 = f32[8,32,1024]{2,1,0:T(8,128)} custom-call(s32[16]{0:T(128)} %old_ids.1, s32[8,6]{1,0:T(8,128)} %nbrs.1, s32[8]{0:T(128)} %refine.1, f32[1,64,512]{2,1,0:T(8,128)} %inverse.1, f32[16,32,1024]{2,1,0:T(8,128)} %u_old.1, f32[16,32,1024]{2,1,0:T(8,128)} %f_old.1, f32[16,32,1024]{2,1,0:T(8,128)} %k_old.1), custom_call_target="tpu_custom_call" | custom-call | tf_op jit(solution)/shard_map/pallas_call | solution.py:827
  49.2 2.3 %copy.9 = f32[8,32,1024]{2,1,0:T(8,128)} copy(f32[8,32,1024]{2,1,0:T(8,128)} %shard_map.73) | data formatting | bytes 2097152

commit v5 on v4

--- a/solution.py
+++ b/solution.py
@@ -64,6 +64,7 @@
     send_out, own_in, recv_out, recv_in, ghosts = [scratch[13 + 2 * i : 15 + 2 * i] for i in range(5)]
     flags, acc, mine, all_sums, rows_e, edge_sums, got_sums, split_sums = scratch[23:31]
     edges = scratch[31:33]
+    result, out_sem = olds[2].at[pl.ds(0, NB)], scratch[46]
     in_sem, move_send, move_recv, out_send, out_recv, inner_send, inner_recv = scratch[33:40]
     flag_send, flag_recv, last_send, last_recv, sum_send, sum_recv = scratch[40:46]
 
@@ -71,6 +72,7 @@
     here = group * members + member
     odd = here % 2 == 1
     even = here % 2 == 0
+    odd_int = here % 2
     has_q = here < devices - 1
     q_stays = jnp.logical_and(odd, has_q)
     p_split = jnp.logical_and(even, here > 0)
@@ -94,7 +96,7 @@
 
     outgoing, incoming = {}, {}
     for s in (0, 1):
-        for axis in range(3):
+        for axis in (2, 1, 0):
             for side in (0, 1):
                 inside, index = around[s][axis][side]
                 exists = inside if s == 0 else both(inside, has_q)
@@ -286,6 +288,10 @@
     ]
 
     def start_exchange(phase, which):
+        @pl.when((p_split, q_stays)[which])
+        def _():
+            inner_copy(phase, which).start()
+
         for (s, axis, side, t), (target, preds) in outgoing.items():
             if s == which:
 
@@ -293,32 +299,30 @@
                 def _():
                     out_copy(phase, s, axis, side, t, target).start()
 
+    def take_exchange(phase, which):
+        for (t, src, axis, side), (source, preds) in incoming.items():
+            if t == which:
+
+                @pl.when(preds[phase])
+                def _():
+                    out_copy(phase, src, axis, 1 - side, t, source).wait_recv()
+
         @pl.when((p_split, q_stays)[which])
         def _():
-            inner_copy(phase, which).start()
-
-    def finish_exchange(phase):
+            inner_copy(phase, 1 - which).wait_recv()
+
+    def end_exchange(phase):
         for (s, axis, side, t), (target, preds) in outgoing.items():
 
             @pl.when(preds[phase])
             def _():
                 out_copy(phase, s, axis, side, t, target).wait_send()
 
-        for (t, src, axis, side), (source, preds) in incoming.items():
-
-            @pl.when(preds[phase])
+        for s, split in enumerate((p_split, q_stays)):
+
+            @pl.when(split)
             def _():
-                out_copy(phase, src, axis, 1 - side, t, source).wait_recv()
-
-        @pl.when(q_stays)
-        def _():
-            inner_copy(phase, 1).wait_send()
-            inner_copy(phase, 0).wait_recv()
-
-        @pl.when(p_split)
-        def _():
-            inner_copy(phase, 0).wait_send()
-            inner_copy(phase, 1).wait_recv()
+                inner_copy(phase, s).wait_send()
 
     def gather_ghosts(phase, t):
         split = (p_split, q_stays)[t]
@@ -540,17 +544,15 @@
 
     def pack_all(field, volume):
         def body(s, carry):
-            pack(0, s, field, volume)
+            pack(0, s, field, volume, inner=False)
             return carry
 
-        lax.fori_loop(0, 2, body, 0)
-
-    def gather_all(phase):
-        gather_ghosts(phase, 0)
-
-        @pl.when(odd)
-        def _():
-            gather_ghosts(phase, 1)
+        pack(0, odd_int, field, volume)
+        lax.fori_loop(1 - odd_int, 2 - odd_int, body, 0)
+
+    def arrive(phase, t):
+        take_exchange(phase, t)
+        gather_ghosts(phase, t)
 
     def to_volume(volume):
         def store(q, tile, part, value):
@@ -603,32 +605,24 @@
         pack(0, 0, 1, k_ref, outer=False)
 
     lax.fori_loop(0, NB, weigh_inside, 0)
-    finish_exchange(0)
-
-    @pl.when(p_split)
-    def _():
-        flag_copy.wait_send()
-
     @pl.when(q_stays)
     def _():
         flag_copy.wait_recv()
 
-    gather_all(0)
-
     @pl.when(odd)
     def _():
+        arrive(0, 1)
         lax.fori_loop(NB, 2 * NB, first_sweep, 0)
         pack(1, 1, 0, u1)
         start_exchange(1, 1)
 
+    arrive(0, 0)
     lax.fori_loop(0, NB, first_sweep, 0)
     pack(1, 0, 0, u1)
     start_exchange(1, 0)
 
     cells = take(sums_of(SOURCE), by_half)
     source_sums = [pick(cells, s, block_of, cell_lane // 2 % 4) for s in (0, 1)]
-    finish_exchange(1)
-    gather_all(1)
 
     def final_copy(p):
         return pltpu.make_async_remote_copy(
@@ -642,6 +636,8 @@
 
     @pl.when(odd)
     def _():
+        arrive(1, 1)
+
         def body(q, carry):
             second_sweep(q, True)
 
@@ -652,6 +648,8 @@
             return carry
 
         lax.fori_loop(NB, 2 * NB, body, 0)
+
+    arrive(1, 0)
 
     def body(q, carry):
         second_sweep(q, False)
@@ -684,7 +682,12 @@
         for p in range(EARLY, MIDDLE):
             final_copy(p).start()
 
-    finish_exchange(2)
+    take_exchange(2, 0)
+
+    @pl.when(odd)
+    def _():
+        take_exchange(2, 1)
+
     totals = []
     for t in (0, 1):
         combined = jnp.zeros((8, LANES), jnp.float32)
@@ -773,12 +776,14 @@
         correction = correction + inverse[0, :, LANES * pair : LANES * (pair + 1)] * vector
     rows_e[...] = jnp.broadcast_to(jnp.sum(correction, axis=1, keepdims=True), (8 * NB, LANES))
 
-    @pl.when(p_split)
-    def _():
-        for p in range(NB):
+    def out_copy_of(p):
+        return pltpu.make_async_copy(result.at[p], out_ref.at[p], out_sem.at[p])
+
+    def finish(p, carry):
+        @pl.when(p_split)
+        def _():
             final_copy(p).wait_recv()
 
-    def finish(p, carry):
         for cell in range(4):
             first = pl.multiple_of(8 * p, 8) + 2 * cell
             lift = jnp.where(depth < EDGE // 2, rows_e[pl.ds(first, 1), :], rows_e[pl.ds(first + 1, 1), :])
@@ -786,10 +791,20 @@
                 for tile in range(4 * (cell % 2), 4 * (cell % 2) + 4):
                     arrived = jnp.where(p_split, final_recv[p, flat(tile, part), :], 0.0)
                     value = u0[p, spot(tile, part), :] + arrived + lift
-                    out_ref[p, 8 * part : 8 * part + 8, LANES * tile : LANES * (tile + 1)] = value
+                    result[p, 8 * part : 8 * part + 8, LANES * tile : LANES * (tile + 1)] = value
+        out_copy_of(p).start()
         return carry
 
     lax.fori_loop(0, NB, finish, 0)
+    for p in range(NB):
+        out_copy_of(p).wait()
+
+    for phase in range(3):
+        end_exchange(phase)
+
+    @pl.when(p_split)
+    def _():
+        flag_copy.wait_send()
 
     @pl.when(even)
     def _():
@@ -823,12 +838,12 @@
     scratch = [pltpu.VMEM(s, jnp.float32) for s in shapes]
     scratch += [dma((3,)), dma((3,)), dma((3,)), dma((3, 2, 6, 2)), dma((3, 2, 2, 6))]
     scratch += [dma((3, 2)), dma((3, 2)), dma, dma, dma((NB,)), dma((NB,))]
-    scratch += [dma((2 * members,)), dma((members,))]
+    scratch += [dma((2 * members,)), dma((members,)), dma((NB,))]
     return pl.pallas_call(
         functools.partial(main_kernel, members, devices),
         out_shape=jax.ShapeDtypeStruct((NB, EDGE, FACE), jnp.float32),
         in_specs=[SM, SM, SM, VM, ANY, ANY, ANY],
-        out_specs=VM,
+        out_specs=ANY,
         scratch_shapes=scratch,
         compiler_params=pltpu.CompilerParams(
             collective_id=1, has_side_effects=True, vmem_limit_bytes=VMEM_LIMIT

time: 51.9 us -> 51.2 us (0.987)
  Pallas kernels: 49.2 us -> 48.6 us
    pallas_call x1, Pallas kernels: 49.2 us -> 48.6 us  [local(): pl.pallas_call(functools.partial(main_kernel, members, devices), out_shap...]
where the time goes in v5:
time: 51.2 us; the launch traced here: 50.9 us
  Pallas kernels  48.6 us (95%)
  local copies, waits for them, and re-layouts  2.31 us (5%)
    pallas_call x1, Pallas kernels, local(): pl.pallas_call(functools.partial(main_kernel, members, devices), out_shap...  48.6 us
    unnamed x1, local copies, waits for them, and re-layouts  2.31 us

profile of v5, /device:TPU:4, one launch (start us, length us, event | category | flops | bytes accessed | tf_op | source)
XLA Modules:
  0.0 50.9 jit_solution(7771748873482983009)
XLA Ops:
  0.0 48.6 %shard_map.73 = f32[8,32,1024]{2,1,0:T(8,128)} custom-call(s32[16]{0:T(128)} %old_ids.1, s32[8,6]{1,0:T(8,128)} %nbrs.1, s32[8]{0:T(128)} %refine.1, f32[1,64,512]{2,1,0:T(8,128)} %inverse.1, f32[16,32,1024]{2,1,0:T(8,128)} %u_old.1, f32[16,32,1024]{2,1,0:T(8,128)} %f_old.1, f32[16,32,1024]{2,1,0:T(8,128)} %k_old.1), custom_call_target="tpu_custom_call" | custom-call | tf_op jit(solution)/shard_map/pallas_call | solution.py:842
  48.6 2.3 %copy.9 = f32[8,32,1024]{2,1,0:T(8,128)} copy(f32[8,32,1024]{2,1,0:T(8,128)} %shard_map.73) | data formatting | bytes 2097152

commit v6 on v5

--- a/solution.py
+++ b/solution.py
@@ -99,24 +99,17 @@
         for axis in (2, 1, 0):
             for side in (0, 1):
                 inside, index = around[s][axis][side]
-                exists = inside if s == 0 else both(inside, has_q)
                 stays = inside if s == 0 else both(inside, q_stays)
                 holder = both(index % 2 == 0, index > 0)
                 for t in (0, 1):
                     target = index if t == 0 else jnp.maximum(index - 1, 0)
-                    first = exists if t == 0 else both(exists, holder)
-                    if s == 1 and t == 0 and axis == 0 and side == 0:
-                        first = both(first, odd)
-                    later = stays if t == 0 else both(stays, holder)
-                    outgoing[s, axis, side, t] = (target, (first, later, later))
+                    pred = stays if t == 0 else both(stays, holder)
+                    outgoing[s, axis, side, t] = (target, pred)
                 receives = inside if s == 0 else both(inside, q_stays)
                 for src in (0, 1):
                     source = index if src == 0 else jnp.maximum(index - 1, 0)
-                    first = receives if src == 0 else both(receives, index > 0)
-                    if s == 0 and src == 1 and axis == 0 and side == 1:
-                        first = both(first, odd)
-                    later = receives if src == 0 else both(receives, holder)
-                    incoming[s, src, axis, side] = (source, (first, later, later))
+                    pred = receives if src == 0 else both(receives, holder)
+                    incoming[s, src, axis, side] = (source, pred)
 
     for b in range(NB):
         flags[NB + b] = jnp.ones((8, LANES), jnp.float32)
@@ -126,11 +119,11 @@
         pl.semaphore_signal(
             barrier, inc=1, device_id={"member": (member + step) % members}, device_id_type=MESH
         )
-    for target, preds in outgoing.values():
-        expected = expected + both(preds[0], target // members != group).astype(jnp.int32)
-    for source, preds in incoming.values():
-
-        @pl.when(both(preds[0], source // members != group))
+    for target, pred in outgoing.values():
+        expected = expected + both(pred, target // members != group).astype(jnp.int32)
+    for source, pred in incoming.values():
+
+        @pl.when(both(pred, source // members != group))
         def _():
             pl.semaphore_signal(barrier, inc=1, device_id=where_is(source), device_id_type=MESH)
 
@@ -292,18 +285,18 @@
         def _():
             inner_copy(phase, which).start()
 
-        for (s, axis, side, t), (target, preds) in outgoing.items():
+        for (s, axis, side, t), (target, pred) in outgoing.items():
             if s == which:
 
-                @pl.when(preds[phase])
+                @pl.when(pred)
                 def _():
                     out_copy(phase, s, axis, side, t, target).start()
 
     def take_exchange(phase, which):
-        for (t, src, axis, side), (source, preds) in incoming.items():
+        for (t, src, axis, side), (source, pred) in incoming.items():
             if t == which:
 
-                @pl.when(preds[phase])
+                @pl.when(pred)
                 def _():
                     out_copy(phase, src, axis, 1 - side, t, source).wait_recv()
 
@@ -312,9 +305,9 @@
             inner_copy(phase, 1 - which).wait_recv()
 
     def end_exchange(phase):
-        for (s, axis, side, t), (target, preds) in outgoing.items():
-
-            @pl.when(preds[phase])
+        for (s, axis, side, t), (target, pred) in outgoing.items():
+
+            @pl.when(pred)
             def _():
                 out_copy(phase, s, axis, side, t, target).wait_send()
 
@@ -331,12 +324,8 @@
                 face = 2 * axis + side
                 total = 0.0
                 for src in (0, 1):
-                    pred = incoming[t, src, axis, side][1][phase]
-                    if phase == 0 and (t, src, axis, side) == (0, 1, 0, 1):
-                        own = jnp.where(even, send_out[0][1, 0], 0.0)
-                        total = total + jnp.where(pred, recv_out[0][t, src, face], own)
-                    else:
-                        total = total + jnp.where(pred, recv_out[phase][t, src, face], 0.0)
+                    pred = incoming[t, src, axis, side][1]
+                    total = total + jnp.where(pred, recv_out[phase][t, src, face], 0.0)
                 ghosts[phase][t, face] = total
                 total = own_in[phase][t, side, axis]
                 if side == t:
@@ -542,14 +531,6 @@
         return block_of + 2**axis * (1 - 2 * bit)
 
 
-    def pack_all(field, volume):
-        def body(s, carry):
-            pack(0, s, field, volume, inner=False)
-            return carry
-
-        pack(0, odd_int, field, volume)
-        lax.fori_loop(1 - odd_int, 2 - odd_int, body, 0)
-
     def arrive(phase, t):
         take_exchange(phase, t)
         gather_ghosts(phase, t)
@@ -564,22 +545,41 @@
         f_ref[q, flat(tile, part), :] = value
 
     settle(0, to_volume(u0))
-    pack_all(0, u0)
+    pack(0, odd_int, 0, u0)
     settle(1, to_volume(k_ref))
-    pack_all(1, k_ref)
+    pack(0, odd_int, 1, k_ref)
     pl.semaphore_wait(barrier, expected)
-    start_exchange(0, 1)
-    start_exchange(0, 0)
-
-    @pl.when(p_split)
-    def _():
-        flag_copy.start()
+    def merge(arrays):
+        def body(p, carry):
+            for tile in range(TILES):
+                for part in range(PARTS):
+                    for i, volume in arrays:
+                        place = flat(tile, part) if i == 2 else spot(tile, part)
+                        volume[p, place, :] += moved[i, p, flat(tile, part), :]
+            return carry
+
+        for i, _ in arrays:
+            moves[i].wait_recv()
+        lax.fori_loop(0, NB, body, 0)
 
     @pl.when(even)
     def _():
+        start_exchange(0, 0)
         moves[0].start()
         moves[1].start()
 
+        @pl.when(p_split)
+        def _():
+            flag_copy.start()
+
+    @pl.when(odd)
+    def _():
+        start_exchange(0, 1)
+        merge(((0, u0), (1, k_ref)))
+        pack(0, 0, 0, u0)
+        pack(0, 0, 1, k_ref)
+        start_exchange(0, 0)
+
     settle(2, to_source)
 
     @pl.when(even)
@@ -589,22 +589,13 @@
     @pl.when(odd)
     def _():
         lax.fori_loop(NB, 2 * NB, weigh_inside, 0)
-        for i in range(3):
-            moves[i].wait_recv()
-
-        def merge(p, carry):
-            for tile in range(TILES):
-                for part in range(PARTS):
-                    for i, volume in enumerate((u0, k_ref)):
-                        volume[p, spot(tile, part), :] += moved[i, p, flat(tile, part), :]
-                    f_ref[p, flat(tile, part), :] += moved[2, p, flat(tile, part), :]
-            return carry
-
-        lax.fori_loop(0, NB, merge, 0)
-        pack(0, 0, 0, u0, outer=False)
-        pack(0, 0, 1, k_ref, outer=False)
 
     lax.fori_loop(0, NB, weigh_inside, 0)
+
+    @pl.when(odd)
+    def _():
+        merge(((2, f_ref),))
+
     @pl.when(q_stays)
     def _():
         flag_copy.wait_recv()
@@ -701,7 +692,7 @@
                 face = 2 * axis + side
                 total = 0.0
                 for src in (0, 1):
-                    pred = incoming[t, src, axis, side][1][2]
+                    pred = incoming[t, src, axis, side][1]
                     total = total + jnp.where(pred, got_sums[t, src, face, row, :], 0.0)
                 outer.append(total)
                 linked.append(combined[face : face + 1, :])

time: 51.2 us -> 49.5 us (0.967)
  Pallas kernels: 48.6 us -> 47 us
    pallas_call x1, Pallas kernels: 48.6 us -> 47 us  [local(): pl.pallas_call(functools.partial(main_kernel, members, devices), out_shap...]
where the time goes in v6:
time: 49.5 us; the launch traced here: 49.3 us
  Pallas kernels  47 us (95%)
  local copies, waits for them, and re-layouts  2.31 us (5%)
    pallas_call x1, Pallas kernels, local(): pl.pallas_call(functools.partial(main_kernel, members, devices), out_shap...  47 us
    unnamed x1, local copies, waits for them, and re-layouts  2.31 us

profile of v6, /device:TPU:4, one launch (start us, length us, event | category | flops | bytes accessed | tf_op | source)
XLA Modules:
  0.0 49.3 jit_solution(2874427157912365761)
XLA Ops:
  0.0 47.0 %shard_map.73 = f32[8,32,1024]{2,1,0:T(8,128)} custom-call(s32[16]{0:T(128)} %old_ids.1, s32[8,6]{1,0:T(8,128)} %nbrs.1, s32[8]{0:T(128)} %refine.1, f32[1,64,512]{2,1,0:T(8,128)} %inverse.1, f32[16,32,1024]{2,1,0:T(8,128)} %u_old.1, f32[16,32,1024]{2,1,0:T(8,128)} %f_old.1, f32[16,32,1024]{2,1,0:T(8,128)} %k_old.1), custom_call_target="tpu_custom_call" | custom-call | tf_op jit(solution)/shard_map/pallas_call | solution.py:833
  47.0 2.3 %copy.9 = f32[8,32,1024]{2,1,0:T(8,128)} copy(f32[8,32,1024]{2,1,0:T(8,128)} %shard_map.73) | data formatting | bytes 2097152

commit v7 on v6

--- a/solution.py
+++ b/solution.py
@@ -18,7 +18,7 @@
 SM = pl.BlockSpec(memory_space=pltpu.SMEM)
 MESH = pl.DeviceIdType.MESH
 FIELDS = (2, 1)
-EARLY, MIDDLE = 4, 6
+EARLY, MIDDLE = 4, 7
 OWN, ALONG_X, ALONG_Y, ALONG_Z, SOURCE = range(5)
 
 
@@ -87,6 +87,7 @@
         pltpu.make_async_copy(ref, olds[i], in_sem.at[i]) for i, ref in enumerate((u_old, k_old, f_old))
     ]
     loads[0].start()
+    loads[1].start()
 
     def both(*preds):
         result = preds[0]
@@ -163,8 +164,8 @@
 
     def settle(i, store):
         loads[i].wait()
-        if i < 2:
-            loads[i + 1].start()
+        if i == 1:
+            loads[2].start()
 
         def own(p, carry):
             slot = jnp.maximum(p - lacking, 0)

time: 49.5 us -> 49.5 us (level)
  the two profiles are of different devices: /device:TPU:4 before, /device:TPU:1 now
where the time goes in v7:
time: 49.5 us; the launch traced here: 49.3 us
  Pallas kernels  47 us (95%)
  local copies, waits for them, and re-layouts  2.31 us (5%)
    pallas_call x1, Pallas kernels, local(): pl.pallas_call(functools.partial(main_kernel, members, devices), out_shap...  47 us
    unnamed x1, local copies, waits for them, and re-layouts  2.31 us

profile of v7, /device:TPU:1, one launch (start us, length us, event | category | flops | bytes accessed | tf_op | source)
XLA Modules:
  0.0 49.3 jit_solution(16892530603990028627)
XLA Ops:
  0.0 47.0 %shard_map.73 = f32[8,32,1024]{2,1,0:T(8,128)} custom-call(s32[16]{0:T(128)} %old_ids.1, s32[8,6]{1,0:T(8,128)} %nbrs.1, s32[8]{0:T(128)} %refine.1, f32[1,64,512]{2,1,0:T(8,128)} %inverse.1, f32[16,32,1024]{2,1,0:T(8,128)} %u_old.1, f32[16,32,1024]{2,1,0:T(8,128)} %f_old.1, f32[16,32,1024]{2,1,0:T(8,128)} %k_old.1), custom_call_target="tpu_custom_call" | custom-call | tf_op jit(solution)/shard_map/pallas_call | solution.py:834
  47.0 2.3 %copy.9 = f32[8,32,1024]{2,1,0:T(8,128)} copy(f32[8,32,1024]{2,1,0:T(8,128)} %shard_map.73) | data formatting | bytes 2097152
